TPU v7x, 32 devices: a whole 2x2x4 slice. The times are simulated.
32 devices in a mesh: row: 8 (over z, x), col: 2 (over y), zs: 2 (over core).
Axes of the slice: x: 2, y: 2, z: 4, core: 2. Of those that a mesh axis runs over, the one named last changes fastest.
Arguments:
- field: bfloat16 [128, 128, 12, 128], P('row', 'col', 'zs'), parts along dimension 2, may hold values from -12 to 12
- norm_gain: float32 [128], replicated, may hold values from 0.5 to 1.5
- first_x: bfloat16 [128, 128], replicated, may hold values from -0.5 to 0.5
- second_x: bfloat16 [128, 256], replicated, may hold values from -0.5 to 0.5
- first_y: bfloat16 [128, 128], replicated, may hold values from -0.5 to 0.5
- second_y: bfloat16 [128, 256], replicated, may hold values from -0.5 to 0.5
- value_weight: bfloat16 [128, 128], replicated, may hold values from -0.5 to 0.5
- out_weight: bfloat16 [128, 128], replicated, may hold values from -0.5 to 0.5
Outputs:
- mixed: bfloat16 [128, 128, 12, 128], P('row', 'col', 'zs'), parts along dimension 2
There are 2 independent parts, one for each index of `zs`. A program takes and returns all parts, laid end to end along the dimension named above; an argument that names none is the same for every part. Nothing has to cross between parts.
All inputs are finite; a program needn't handle non-finite values.
Results may differ from a plain program's by a relative error of at most 0.006.
Values may be sent and summed in bfloat16 or wider, within the bound.
No kernel may reach another device: no remote copies, remote signals or barrier semaphores. Data moves between devices by JAX's collectives and lax.ppermute only.
A program may use at most 64 MiB of HBM per device.

v0:
```python
import jax
import jax.numpy as jnp
from jax import lax
from jax.sharding import PartitionSpec as P

H = 8


EPS = 1e-05
HIGH = lax.Precision.HIGHEST


def normalize(slab, gain):
    values = slab.astype(jnp.float32)
    center = jnp.mean(values, axis=-1, keepdims=True)
    spread = jnp.mean((values - center) ** 2, axis=-1, keepdims=True)
    return ((values - center) * lax.rsqrt(spread + EPS) * gain).astype(jnp.bfloat16)


def project(normed, w_first, w_second):
    hidden = jax.nn.gelu(jnp.dot(normed, w_first, preferred_element_type=jnp.float32)).astype(
        jnp.bfloat16
    )
    return jnp.dot(hidden, w_second, preferred_element_type=jnp.float32)


def body(field, norm_gain, first_x, second_x, first_y, second_y, value_weight, out_weight):
    x_local, y_local, z_local, width = field.shape
    heads = H
    depth = width // heads
    total_x = x_local * lax.axis_size("row")
    total_y = y_local * lax.axis_size("col")
    normed = normalize(field, norm_gain)
    part_x = jnp.sum(project(normed, first_x, second_x), axis=(1, 2))
    part_y = jnp.sum(project(normed, first_y, second_y), axis=(0, 2))
    summary_x = lax.psum(part_x, "col") / (total_y * z_local)
    summary_y = lax.psum(part_y, "row") / (total_x * z_local)
    value = jnp.dot(normed, value_weight, preferred_element_type=jnp.float32).astype(jnp.bfloat16)
    query_x, key_x = (summary_x[:, :width], summary_x[:, width:])
    query_y, key_y = (summary_y[:, :width], summary_y[:, width:])
    scale_x = jnp.sqrt(jnp.float32(total_x))
    scale_y = jnp.sqrt(jnp.float32(total_y))
    every_qx, every_kx = (
        lax.all_gather(query_x, "row", axis=0, tiled=True),
        lax.all_gather(key_x, "row", axis=0, tiled=True),
    )
    every_qy, every_ky = (
        lax.all_gather(query_y, "col", axis=0, tiled=True),
        lax.all_gather(key_y, "col", axis=0, tiled=True),
    )
    block = lax.all_to_all(value, "row", split_axis=1, concat_axis=0, tiled=True)
    lines = block.reshape(block.shape[:3] + (heads, depth)).astype(jnp.float32)
    s_x = jnp.einsum("xhd,xyzhe->yzhde", every_kx.reshape(-1, heads, depth), lines, precision=HIGH)
    result = (
        jnp.einsum("xhd,yzhde->xyzhe", every_qx.reshape(-1, heads, depth), s_x, precision=HIGH)
        / scale_x
    )
    result = result.reshape(block.shape)
    u_x = lax.all_to_all(result, "row", split_axis=0, concat_axis=1, tiled=True)
    block = lax.all_to_all(u_x, "col", split_axis=0, concat_axis=1, tiled=True)
    lines = block.reshape(block.shape[:3] + (heads, depth))
    s_y = jnp.einsum("yhd,xyzhe->xzhde", every_ky.reshape(-1, heads, depth), lines, precision=HIGH)
    result = (
        jnp.einsum("yhd,xzhde->xyzhe", every_qy.reshape(-1, heads, depth), s_y, precision=HIGH)
        / scale_y
    )
    result = result.astype(jnp.bfloat16).reshape(block.shape)
    u_y = lax.all_to_all(result, "col", split_axis=1, concat_axis=0, tiled=True)
    return jnp.dot(u_y, out_weight, preferred_element_type=jnp.float32).astype(jnp.bfloat16)


def solution(mesh):
    placed = (P("row", "col", "zs", None), P(), P(), P(), P(), P(), P(), P())
    return jax.shard_map(
        body, mesh=mesh, in_specs=placed, out_specs=P("row", "col", "zs", None), check_vma=False
    )
```

profile of v0, /device:TPU:0, one launch (start us, length us, event | category | flops | bytes accessed | tf_op | source)
XLA Modules:
  0.0 355.3 jit_solution(5366305813154999806)
XLA Ops:
  6.5 0.0 copy-start
  6.5 2.4 convert_reduce_fusion
  9.0 3.0 fusion.4
  12.0 0.0 copy-done.1
  12.0 0.0 copy-done.7
  12.0 0.0 copy-done.4
  12.0 2.4 convolution_convert_fusion.1
  14.4 0.0 copy-start.3
  14.4 0.0 copy-start.5
  14.4 2.2 copy.43
  16.6 7.3 %all-to-all-start = ((bf16[16,64,6,128]{3,0,2,1:T(8,128)(2,1)}), bf16[16,64,6,128]{3,0,2,1:T(8,128)(2,1)S(1)}, u32[]{:S(2)}, u32[]{:S(2)}) async-start(bf16[16,64,6,128]{3,0,2,1:T(8,128)(2,1)} %copy.43), calls=%async_computation | async-start | bytes 3145728 | tf_op jit(solution)/shard_map/all_to_all | solution.py:51
  23.9 0.0 copy-done.3
  23.9 2.5 convolution_reduce_fusion.1
  26.4 8.2 %psum.14 = f32[16,256]{1,0:T(8,128)S(1)} all-reduce(f32[16,256]{1,0:T(8,128)S(1)} %convolution_reduce_fusion.1), channel_id=1, replica_groups=mesh['row'=8,'col'=2,'zs'=2] {'col'}, use_global_device_ids=true, to_apply=%region_3.0 | all-reduce | flops 4096 | bytes 32768 | tf_op jit(solution)/shard_map/psum | solution.py:36
  34.6 46.3 %all_gather.12 = f32[128,128]{1,0:T(8,128)S(1)} all-gather(f32[16,128]{1,0:T(8,128)S(1)} %get-tuple-element.7), channel_id=1, replica_groups=mesh['row'=8,'col'=2,'zs'=2] {'row'}, dimensions={0}, use_global_device_ids=true | all-gather | bytes 73728 | tf_op jit(solution)/shard_map/all_gather | solution.py:45
  80.9 0.1 copy.45
  81.0 30.5 %all_gather.13 = f32[128,128]{1,0:T(8,128)S(1)} all-gather(f32[16,128]{1,0:T(8,128)S(1)} %get-tuple-element.8), channel_id=1, replica_groups=mesh['row'=8,'col'=2,'zs'=2] {'row'}, dimensions={0}, use_global_device_ids=true | all-gather | bytes 73728 | tf_op jit(solution)/shard_map/all_gather | solution.py:44
  111.5 0.1 copy.47
  111.6 0.0 all-to-all-done
  111.6 0.6 copy.77
  112.2 10.8 %reshape.39 = bf16[128,8,6,8,16]{4,3,1,2,0:T(8,128)(2,1)} reshape(bf16[8,16,8,6,128]{4,2,3,1,0:T(8,128)(2,1)S(1)} %bitcast.102) | data formatting | bytes 3145728 | tf_op jit(solution)/shard_map/reshape | solution.py:52
  123.1 27.4 %fusion = f32[8,8,6,16,16]{4,3,2,1,0:T(8,128)S(1)} fusion(f32[128,8,16,1,1]{0,2,4,3,1:T(8,128)S(1)} %bitcast.106, bf16[128,8,6,8,16]{4,3,1,2,0:T(8,128)(2,1)} %reshape.39), kind=kOutput, calls=%fused_computation | convolution fusion | flops 150994944 | bytes 2031616 | tf_op jit(solution)/shard_map/xhd,xyzhe->yzhde/dot_general | solution.py:53
  150.5 3.1 multiply_bitcast_fusion
  153.6 0.4 copy.48
  154.0 2.6 copy.49
  156.6 63.2 %all_to_all.66 = f32[128,8,6,128]{3,1,2,0:T(8,128)S(1)} all-to-all(f32[128,8,6,128]{3,1,2,0:T(8,128)} %copy.49), channel_id=1, replica_groups=mesh['row'=8,'col'=2,'zs'=2] {'row'}, dimensions={0} | all-to-all | bytes 6291456 | tf_op jit(solution)/shard_map/all_to_all | solution.py:59
  219.8 2.1 copy.76
  221.9 4.1 %all-to-all-start.2 = ((f32[16,64,6,128]{3,1,2,0:T(8,128)}), f32[16,64,6,128]{3,1,2,0:T(8,128)S(1)}, u32[]{:S(2)}, u32[]{:S(2)}) async-start(f32[16,64,6,128]{3,1,2,0:T(8,128)} %bitcast.95), calls=%async_computation.2 | async-start | bytes 6291456 | tf_op jit(solution)/shard_map/all_to_all | solution.py:60
  226.0 0.0 all-reduce.2.cloned.1.call-start
  226.0 4.3 %convolution_reduce_fusion = f32[64,256]{1,0:T(8,128)} fusion(bf16[16,64,6,128]{3,1,2,0:T(8,128)(2,1)} %param.8, f32[128]{0:T(128)S(1)} %copy-done.7, f32[16,64,6]{1,2,0:T(8,128)S(1)} %add_rsqrt_fusion, f32[16,64,6]{1,2,0:T(8,128)S(1)} %broadcast_multiply_fusion.1, bf16[128,256]{1,0:T(8,128)(2,1)S(1)} %copy-done, bf16[128,128]{1,0:T(8,128)(2,1)S(1)} %copy-done.6), kind=kOutput, calls=%fused_computation.36 | convolution fusion | flops 616546304 | bytes 1786368 | tf_op jit(solution)/shard_map/dot_general | solution.py:24
  230.3 0.0 all-reduce.2.cloned.1.call-update
  230.3 68.2 %all-reduce.2.cloned.1.call-done = f32[64,256]{1,0:T(8,128)} async-done(((f32[64,256]{1,0:T(8,128)}), f32[64,256]{1,0:T(8,128)}) %all-reduce.2.cloned.1.call-update) | async-done | bytes 65552 | tf_op jit(solution)/shard_map/psum | solution.py:37
  298.5 0.8 broadcast_multiply_fusion
  299.4 4.6 %all_gather.14 = f32[128,128]{1,0:T(8,128)S(1)} all-gather(f32[64,128]{1,0:T(8,128)S(1)} %get-tuple-element.5), channel_id=1, replica_groups=mesh['row'=8,'col'=2,'zs'=2] {'col'}, dimensions={0}, use_global_device_ids=true | all-gather | bytes 98304 | tf_op jit(solution)/shard_map/all_gather | solution.py:49
  304.0 0.1 copy.52
  304.1 4.6 %all_gather.15 = f32[128,128]{1,0:T(8,128)S(1)} all-gather(f32[64,128]{1,0:T(8,128)S(1)} %get-tuple-element.6), channel_id=1, replica_groups=mesh['row'=8,'col'=2,'zs'=2] {'col'}, dimensions={0}, use_global_device_ids=true | all-gather | bytes 98304 | tf_op jit(solution)/shard_map/all_gather | solution.py:48
  308.7 0.1 copy.54
  308.8 0.0 all-to-all-done.2
  308.8 6.4 %copy.51 = f32[2,8,64,6,128]{2,0,4,3,1:T(2,128)} copy(f32[2,8,64,6,128]{4,2,3,1,0:T(8,128)S(1)} %bitcast.100) | data formatting | bytes 6291456 | tf_op jit(solution)/shard_map/all_to_all | solution.py:60
  315.2 5.8 %reshape.43 = f32[8,128,6,8,16]{1,4,3,2,0:T(8,128)S(1)} reshape(f32[8,2,64,6,128]{2,1,4,3,0:T(2,128)} %bitcast.97) | data formatting | bytes 6291456 | tf_op jit(solution)/shard_map/reshape | solution.py:61
  321.1 2.9 fusion.27
  324.0 3.0 fusion.33
  327.0 0.5 copy.55
  327.4 1.0 copy.56
  328.5 0.0 copy-start.2
  328.5 17.9 %all_to_all.67 = bf16[8,128,6,128]{3,0,2,1:T(8,128)(2,1)S(1)} all-to-all(bf16[8,128,6,128]{3,0,2,1:T(8,128)(2,1)S(1)} %copy.56), channel_id=1, replica_groups=mesh['row'=8,'col'=2,'zs'=2] {'col'}, dimensions={1} | all-to-all | bytes 3145728 | tf_op jit(solution)/shard_map/all_to_all | solution.py:68
  346.3 0.4 copy.58
  346.8 1.7 convolution_convert_fusion
  (13 shorter events, 0.1 us)
Async XLA Ops:
  6.5 219.5 %copy-start = (bf16[128,256]{1,0:T(8,128)(2,1)S(1)}, bf16[128,256]{1,0:T(8,128)(2,1)}, u32[]{:S(2)}) copy-start(bf16[128,256]{1,0:T(8,128)(2,1)} %param.13) | copy-start | bytes 196612
  6.5 5.4 %copy-start.1 = (bf16[16,64,6,128]{3,1,2,0:T(8,128)(2,1)S(1)}, bf16[16,64,6,128]{3,1,2,0:T(8,128)(2,1)}, u32[]{:S(2)}) copy-start(bf16[16,64,6,128]{3,1,2,0:T(8,128)(2,1)} %param.8) | copy-start | bytes 4718596
  6.5 5.4 %copy-start.7 = (f32[128]{0:T(128)S(1)}, f32[128]{0:T(128)}, u32[]{:S(2)}) copy-start(f32[128]{0:T(128)} %param.9) | copy-start | bytes 1540
  6.5 5.4 %copy-start.4 = (bf16[128,128]{1,0:T(8,128)(2,1)S(1)}, bf16[128,128]{1,0:T(8,128)(2,1)}, u32[]{:S(2)}) copy-start(bf16[128,128]{1,0:T(8,128)(2,1)} %param.14) | copy-start | bytes 98308
  14.4 9.4 %copy-start.3 = (bf16[128,256]{1,0:T(8,128)(2,1)S(1)}, bf16[128,256]{1,0:T(8,128)(2,1)}, u32[]{:S(2)}) copy-start(bf16[128,256]{1,0:T(8,128)(2,1)} %param.11) | copy-start | bytes 196612
  14.4 9.4 %copy-start.5 = (bf16[128,128]{1,0:T(8,128)(2,1)S(1)}, bf16[128,128]{1,0:T(8,128)(2,1)}, u32[]{:S(2)}) copy-start(bf16[128,128]{1,0:T(8,128)(2,1)} %param.10) | copy-start | bytes 98308
  16.6 95.0 %all-to-all-start = ((bf16[16,64,6,128]{3,0,2,1:T(8,128)(2,1)}), bf16[16,64,6,128]{3,0,2,1:T(8,128)(2,1)S(1)}, u32[]{:S(2)}, u32[]{:S(2)}) async-start(bf16[16,64,6,128]{3,0,2,1:T(8,128)(2,1)} %copy.43), calls=%async_computation | async-start | bytes 3145728 | tf_op jit(solution)/shard_map/all_to_all | solution.py:51
  221.9 4.1 %copy-start.6 = (bf16[128,128]{1,0:T(8,128)(2,1)S(1)}, bf16[128,128]{1,0:T(8,128)(2,1)}, u32[]{:S(2)}) copy-start(bf16[128,128]{1,0:T(8,128)(2,1)} %param.12) | copy-start | bytes 98308
  221.9 86.9 %all-to-all-start.2 = ((f32[16,64,6,128]{3,1,2,0:T(8,128)}), f32[16,64,6,128]{3,1,2,0:T(8,128)S(1)}, u32[]{:S(2)}, u32[]{:S(2)}) async-start(f32[16,64,6,128]{3,1,2,0:T(8,128)} %bitcast.95), calls=%async_computation.2 | async-start | bytes 6291456 | tf_op jit(solution)/shard_map/all_to_all | solution.py:60
  226.0 72.6 %all-reduce.2.cloned.1.call-start = ((), (), s32[]{:S(2)}) async-start(), calls=%async_computation.4 | async-start | bytes 131072 | tf_op jit(solution)/shard_map/psum | solution.py:37
  328.5 18.3 %copy-start.2 = (bf16[128,128]{1,0:T(8,128)(2,1)S(1)}, bf16[128,128]{1,0:T(8,128)(2,1)}, u32[]{:S(2)}) copy-start(bf16[128,128]{1,0:T(8,128)(2,1)} %param.15) | copy-start | bytes 98308
Sparse Core Ops, SparseCore 0:
  230.4 68.0 all-reduce.1
where the time goes:
time: 356 us; the launch traced here: 355 us
  blocking collectives  175 us (49%)
  waiting for transfers between devices  68.2 us (19%)
  matrix products  47.3 us (13%)
  local copies, waits for them, and re-layouts  33.3 us (9%)
  between operations  13.7 us (4%)
  starting transfers between devices  11.4 us (3%)
  other arithmetic  6.24 us (2%)
    psum x1, waiting for transfers between devices, body(): summary_y = lax.psum(part_y, 'row') / (total_x * z_local)  68.2 us
    all_to_all x1, blocking collectives, body(): u_x = lax.all_to_all(result, 'row', split_axis=0, concat_axis=1, tiled=True)  63.2 us
    all_gather x1, blocking collectives, body(): lax.all_gather(key_x, 'row', axis=0, tiled=True)  46.3 us
    all_gather x1, blocking collectives, body(): lax.all_gather(query_x, 'row', axis=0, tiled=True)  30.5 us
    dot_general x1, matrix products, body(): jnp.einsum('xhd,xyzhe->yzhde', every_kx.reshape(-1, heads, depth), lines,...  27.4 us
    all_to_all x1, blocking collectives, body(): u_y = lax.all_to_all(result, 'col', split_axis=1, concat_axis=0, tiled=True)  17.9 us
    reshape x1, local copies, waits for them, and re-layouts, body(): lines = block.reshape(block.shape[:3] + (heads, depth)).astype(jnp.float32)  10.8 us
    psum x1, blocking collectives, body(): summary_x = lax.psum(part_x, 'col') / (total_y * z_local)  8.18 us
  transfers between devices with their start and end apart: 3, of which 1 were waited for; matrix products, arithmetic and copies ran while one was open for 2% of the time, Pallas kernels for 0%

commit v1 on v0

v1 whole, which is shorter than its diff:
```python
import functools

import jax
import jax.numpy as jnp
from jax import lax
from jax.experimental import pallas as pl
from jax.experimental.pallas import tpu as pltpu
from jax.sharding import PartitionSpec as P

H = 8
EPS = 1e-05
HIGH = lax.Precision.HIGHEST
F32 = jnp.float32
BF16 = jnp.bfloat16
GELU_A = 0.7978845608028654
GELU_B = GELU_A * 0.044715
VMEM_LIMIT = 48 * 1024 * 1024


def dot(a, b):
    return jnp.dot(a, b, preferred_element_type=F32)


def halves(a):
    high = a.astype(BF16)
    return high, (a - high.astype(F32)).astype(BF16)


def spread(rows, depth):
    width = rows.shape[1]
    shape = (width, depth * width)
    source = lax.broadcasted_iota(jnp.int32, shape, 0)
    target = lax.broadcasted_iota(jnp.int32, shape, 1)
    lane = target % width
    pick = (source // depth == lane // depth) & (source % depth == target // width)
    return jnp.dot(rows, pick.astype(F32), precision=HIGH, preferred_element_type=F32)


def pooled_kernel(field_ref, gain_ref, first_ref, weight_ref, sum_x_ref, sum_y_ref, value_ref):
    x_local, z_local, y_local, width = field_ref.shape
    ones = jnp.full((width, width), 1.0 / width, BF16)
    ones_two = jnp.full((2 * width, width), 1.0 / width, BF16)
    gain = gain_ref[...]
    sum_y_ref[...] = jnp.zeros_like(sum_y_ref)

    def step(i, carry):
        slab = field_ref[i].reshape(z_local * y_local, width)
        centred = slab.astype(F32) - dot(slab, ones)
        high, low = halves(centred * centred)
        spread_ = dot(jnp.concatenate([high, low], axis=1), ones_two)
        normed = (centred * lax.rsqrt(spread_ + EPS) * gain).astype(BF16)
        h = dot(normed, first_ref[...])
        g = h + h * jnp.tanh(h * (GELU_A + GELU_B * (h * h)))
        sum_x_ref[pl.ds(i, 1), :] = jnp.sum(g[:, :width], axis=0, keepdims=True)
        sum_y_ref[...] += jnp.sum(g[:, width:].reshape(z_local, y_local, width), axis=0)
        value = dot(normed, weight_ref[...]).astype(BF16)
        for z in range(z_local):
            value_ref[i, :, z * width : (z + 1) * width] = value[z * y_local : (z + 1) * y_local]
        return carry

    lax.fori_loop(0, x_local, step, 0)


def outer_kernel(scale_x, scale_y, sum_x_ref, sum_y_ref, key_x_ref, key_y_ref, value_ref, total_ref, part_ref):
    x_local, y_local, lanes = value_ref.shape
    width = key_x_ref.shape[0]
    depth = width // H
    key_x = jnp.dot(sum_x_ref[...] * scale_x, key_x_ref[...].astype(F32), precision=HIGH)
    key_y = jnp.dot(sum_y_ref[...] * scale_y, key_y_ref[...].astype(F32), precision=HIGH)
    high, low = halves(key_y.T)
    left = jnp.concatenate([high, low], axis=0)
    spread_x = spread(key_x, depth)
    head = (lax.broadcasted_iota(jnp.int32, (depth, lanes), 1) % width) // depth

    for i in range(x_local):
        both = dot(left, value_ref[i])
        both = both[:width] + both[width:]
        acc = both[:depth]
        for h in range(1, H):
            acc = jnp.where(head == h, both[h * depth : (h + 1) * depth], acc)
        part_ref[i] = acc

    for d in range(depth):
        for z in range(lanes // width):
            cols = slice(z * width, (z + 1) * width)
            acc = jnp.zeros((depth, width), F32)
            for i in range(x_local):
                acc += spread_x[i : i + 1, d * width : (d + 1) * width] * part_ref[i, :, cols]
            total_ref[d * depth : (d + 1) * depth, cols] = acc.astype(BF16)


def finish_kernel(scale_x, scale_y, sum_x_ref, sum_y_ref, query_x_ref, query_y_ref, total_ref, weight_ref, out_ref):
    x_local, z_local, y_local, width = out_ref.shape
    depth = width // H
    lanes = z_local * width
    query_x = jnp.dot(sum_x_ref[...] * scale_x, query_x_ref[...].astype(F32), precision=HIGH)
    query_y = jnp.dot(sum_y_ref[...] * scale_y, query_y_ref[...].astype(F32), precision=HIGH)
    high, low = halves(query_y)
    left = jnp.concatenate([high, low, high], axis=1)
    spread_x = spread(query_x, depth)
    head = (lax.broadcasted_iota(jnp.int32, (depth, lanes), 1) % width) // depth
    zero = jnp.zeros((depth, lanes), BF16)

    for i in range(x_local):
        pieces = []
        for z in range(z_local):
            cols = slice(z * width, (z + 1) * width)
            acc = jnp.zeros((depth, width), F32)
            for d in range(depth):
                acc += spread_x[i : i + 1, d * width : (d + 1) * width] * total_ref[
                    d * depth : (d + 1) * depth, cols
                ].astype(F32)
            pieces.append(acc)
        w_high, w_low = halves(jnp.concatenate(pieces, axis=1))
        diag_high = jnp.concatenate([jnp.where(head == h, w_high, zero) for h in range(H)], axis=0)
        diag_low = jnp.concatenate([jnp.where(head == h, w_low, zero) for h in range(H)], axis=0)
        u = dot(left, jnp.concatenate([diag_high, diag_high, diag_low], axis=0)).astype(BF16)
        for z in range(z_local):
            out_ref[i, z] = dot(u[:, z * width : (z + 1) * width], weight_ref[...]).astype(BF16)


def call(kernel, out_shape, flops, scratch=()):
    return pl.pallas_call(
        kernel,
        out_shape=out_shape,
        scratch_shapes=list(scratch),
        compiler_params=pltpu.CompilerParams(vmem_limit_bytes=VMEM_LIMIT),
        cost_estimate=pl.CostEstimate(flops=flops, bytes_accessed=4 << 20, transcendentals=0),
    )


def pair_sum(value, axis):
    size = lax.axis_size(axis)
    bit = 1
    while bit < size:
        value = value + lax.ppermute(value, axis, [(i, i ^ bit) for i in range(size)])
        bit *= 2
    return value


def total_sum(part):
    axes = ("row", "col")
    n = lax.axis_size("row") * lax.axis_size("col")
    rows, lanes = part.shape
    blocks = lax.all_to_all(part.reshape(n, rows // n, lanes), axes, 0, 0)
    mine = jnp.sum(blocks.astype(F32), axis=0).astype(BF16)
    spread_ = jnp.broadcast_to(mine, blocks.shape)
    return lax.all_to_all(spread_, axes, 0, 0).reshape(rows, lanes)


def body(field, norm_gain, first_x, second_x, first_y, second_y, value_weight, out_weight):
    x_local, y_local, z_local, width = field.shape
    depth = width // H
    lanes = z_local * width
    total_x = x_local * lax.axis_size("row")
    total_y = y_local * lax.axis_size("col")
    sum_x, sum_y, value = call(
        pooled_kernel,
        [
            jax.ShapeDtypeStruct((x_local, width), F32),
            jax.ShapeDtypeStruct((y_local, width), F32),
            jax.ShapeDtypeStruct((x_local, y_local, lanes), BF16),
        ],
        1 << 30,
    )(
        jnp.transpose(field, (0, 2, 1, 3)),
        norm_gain.reshape(1, width),
        jnp.concatenate([first_x, first_y], axis=1),
        value_weight,
    )
    sum_x = pair_sum(sum_x, "col")
    sum_y = pair_sum(sum_y, "row")
    mean_x = 0.5 / (total_y * z_local)
    mean_y = 0.5 / (total_x * z_local)
    part = call(
        functools.partial(outer_kernel, mean_x, mean_y),
        jax.ShapeDtypeStruct((depth * depth, lanes), BF16),
        1 << 30,
        [pltpu.VMEM((x_local, depth, lanes), F32)],
    )(sum_x, sum_y, second_x[:, width:], second_y[:, width:], value)
    total = total_sum(part)
    out = call(
        functools.partial(finish_kernel, mean_x * total_x**-0.5, mean_y * total_y**-0.5),
        jax.ShapeDtypeStruct((x_local, z_local, y_local, width), BF16),
        1 << 30,
    )(sum_x, sum_y, second_x[:, :width], second_y[:, :width], total, out_weight)
    return jnp.transpose(out, (0, 2, 1, 3))


def solution(mesh):
    placed = (P("row", "col", "zs", None), P(), P(), P(), P(), P(), P(), P())
    return jax.shard_map(
        body, mesh=mesh, in_specs=placed, out_specs=P("row", "col", "zs", None), check_vma=False
    )
```

time: 356 us -> 65.2 us (0.18)
  blocking collectives: 175 us -> 30.1 us
  waiting for transfers between devices: 68.2 us -> 4.1 us
  matrix products: 47.3 us -> 0 us
  local copies, waits for them, and re-layouts: 33.3 us -> 2.88 us
  Pallas kernels: 0 us -> 17.1 us
  between operations: 13.7 us -> 0.07 us
  other arithmetic: 6.24 us -> 0.86 us
    all_gather x4 -> x0, blocking collectives: 86 us -> none  [the longest x1 46.3 us: body(): lax.all_gather(key_x, 'row', axis=0, tiled=True)]
    psum x1 -> x0, waiting for transfers between devices: 68.2 us -> none  [body(): summary_y = lax.psum(part_y, 'row') / (total_x * z_local)]
    all_to_all x2, blocking collectives: 81 us -> 30.1 us  [the longest x1 16.9 us: total_sum(): blocks = lax.all_to_all(part.reshape(n, rows // n, lanes), axes, 0, 0)]
    dot_general x8 -> x0, matrix products: 47.3 us -> none  [the longest x1 27.4 us: body(): jnp.einsum('xhd,xyzhe->yzhde', every_kx.reshape(-1, heads, depth), lines,...]
    reshape x4 -> x0, local copies, waits for them, and re-layouts: 20.3 us -> none  [the longest x1 10.8 us: body(): lines = block.reshape(block.shape[:3] + (heads, depth)).astype(jnp.float32)]
    pallas_call x0 -> x3, Pallas kernels: none -> 17.1 us  [the longest x1 8.07 us: body(): call(pooled_kernel, [jax.ShapeDtypeStruct((x_local, width), F32), jax.Sha...]
    all_to_all x2 -> x0, starting transfers between devices: 11.3 us -> none  [the longest x1 7.25 us: body(): lax.all_to_all(value, 'row', split_axis=1, concat_axis=0, tiled=True)]
    ppermute x0 -> x4, starting transfers between devices: none -> 9.66 us  [pair_sum(): lax.ppermute(value, axis, [(i, i ^ bit) for i in range(size)])]
  transfers between devices with their start and end apart: 3 -> 4, of which waited for: 1 -> 3; matrix products, arithmetic and copies ran while one was open for 2% -> 0% of each run, Pallas kernels for 0% -> 0%
where the time goes in v1:
time: 65.2 us; the launch traced here: 64.7 us
  blocking collectives  30.1 us (46%)
  Pallas kernels  17.1 us (26%)
  starting transfers between devices  9.66 us (15%)
  waiting for transfers between devices  4.1 us (6%)
  local copies, waits for them, and re-layouts  2.88 us (4%)
  other arithmetic  0.86 us (1%)
    all_to_all x1, blocking collectives, total_sum(): blocks = lax.all_to_all(part.reshape(n, rows // n, lanes), axes, 0, 0)  16.9 us
    all_to_all x1, blocking collectives, total_sum(): return lax.all_to_all(spread_, axes, 0, 0).reshape(rows, lanes)  13.2 us
    ppermute x4, starting transfers between devices, pair_sum(): lax.ppermute(value, axis, [(i, i ^ bit) for i in range(size)])  9.66 us
    pallas_call x1, Pallas kernels, body(): call(pooled_kernel, [jax.ShapeDtypeStruct((x_local, width), F32), jax.Sha...  8.07 us
    pallas_call x1, Pallas kernels, body(): call(functools.partial(finish_kernel, mean_x * total_x ** (-0.5), mean_y...  6.28 us
    ppermute x4, waiting for transfers between devices, pair_sum(): lax.ppermute(value, axis, [(i, i ^ bit) for i in range(size)])  4.1 us
    unnamed x12, local copies, waits for them, and re-layouts  2.83 us
    pallas_call x1, Pallas kernels, body(): call(functools.partial(outer_kernel, mean_x, mean_y), jax.ShapeDtypeStruc...  2.71 us
  transfers between devices with their start and end apart: 4, of which 3 were waited for; matrix products, arithmetic and copies ran while one was open for 0% of the time, Pallas kernels for 0%

profile of v1, /device:TPU:0, one launch (start us, length us, event | category | flops | bytes accessed | tf_op | source)
XLA Modules:
  0.0 64.7 jit_solution(9768043514745453126)
XLA Ops:
  0.0 0.8 %pad_maximum_fusion.first_ref = bf16[128,256]{1,0:T(8,128)(2,1)S(1)} fusion(bf16[128,128]{1,0:T(8,128)(2,1)} %param.12, bf16[128,128]{1,0:T(8,128)(2,1)} %param.10), kind=kLoop, calls=%fused_computation | loop fusion | flops 131072 | bytes 131072 | tf_op jit(solution)/shard_map/concatenate | solution.py:168
  0.8 0.0 copy-start
  0.8 1.4 %copy-done = bf16[16,64,6,128]{3,1,2,0:T(8,128)(2,1)S(1)} copy-done((bf16[16,64,6,128]{3,1,2,0:T(8,128)(2,1)S(1)}, bf16[16,64,6,128]{3,1,2,0:T(8,128)(2,1)}, u32[]{:S(2)}) %copy-start) | copy-done | bytes 1572888
  2.2 0.0 copy-start.1
  2.2 0.8 %copy-done.1 = bf16[128,128]{1,0:T(8,128)(2,1)S(1)} copy-done((bf16[128,128]{1,0:T(8,128)(2,1)S(1)}, bf16[128,128]{1,0:T(8,128)(2,1)}, u32[]{:S(2)}) %copy-start.1) | copy-done | bytes 32792
  3.0 0.0 copy-start.3
  3.0 0.7 %copy-done.3 = f32[128]{0:T(128)S(1)} copy-done((f32[128]{0:T(128)S(1)}, f32[128]{0:T(128)}, u32[]{:S(2)}) %copy-start.3) | copy-done | bytes 536
  3.6 0.0 copy-start.4
  3.6 0.0 copy-start.5
  3.6 8.1 %shard_map.82 = (f32[16,128]{1,0:T(8,128)S(1)}, f32[64,128]{1,0:T(8,128)S(1)}, bf16[16,64,768]{2,1,0:T(8,128)(2,1)S(1)}) custom-call(bf16[16,6,64,128]{3,2,1,0:T(8,128)(2,1)S(1)} %bitcast.7, f32[1,128]{1,0:T(1,128)S(1)} %bitcast.8, bf16[128,256]{1,0:T(8,128)(2,1)S(1)} %pad_maximum_fusion.first_ref, bf16[128,128]{1,0:T(8,128)(2,1)S(1)} %copy-done.1), custom_call_target="tpu_custom_call" | custom-call | flops 1073741824 | bytes 4194304 | tf_op jit(solution)/shard_map/pallas_call | solution.py:157
  11.7 3.0 %collective-permute-start.1 = (f32[64,128]{1,0:T(8,128)S(1)}, f32[64,128]{1,0:T(8,128)S(1)}, u32[]{:S(2)}, u32[]{:S(2)}) collective-permute-start(f32[64,128]{1,0:T(8,128)S(1)} %get-tuple-element.9), channel_id=1, source_target_pairs={{0,4},{4,0},{8,12},{12,8},{16,20},{20,16},{24,28},{28,24},{1,5},{5... | collective-permute-start | bytes 98312 | tf_op jit(solution)/shard_map/ppermute | solution.py:136
  14.7 1.9 %collective-permute-done.1 = f32[64,128]{1,0:T(8,128)S(1)} collective-permute-done((f32[64,128]{1,0:T(8,128)S(1)}, f32[64,128]{1,0:T(8,128)S(1)}, u32[]{:S(2)}, u32[]{:S(2)}) %collective-permute-start.1) | collective-permute-done | bytes 32800 | tf_op jit(solution)/shard_map/ppermute | solution.py:136
  16.6 2.1 %collective-permute-start.2 = (f32[64,128]{1,0:T(8,128)S(1)}, f32[64,128]{1,0:T(8,128)S(1)}, u32[]{:S(2)}, u32[]{:S(2)}) collective-permute-start(f32[64,128]{1,0:T(8,128)S(1)} %add.13), channel_id=1, source_target_pairs={{0,8},{4,12},{8,0},{12,4},{16,24},{20,28},{24,16},{28,20},{1,9},{5... | collective-permute-start | bytes 98312 | tf_op jit(solution)/shard_map/ppermute | solution.py:136
  18.7 1.5 %collective-permute-start = (f32[16,128]{1,0:T(8,128)S(1)}, f32[16,128]{1,0:T(8,128)S(1)}, u32[]{:S(2)}, u32[]{:S(2)}) collective-permute-start(f32[16,128]{1,0:T(8,128)S(1)} %get-tuple-element.8), channel_id=1, source_target_pairs={{0,2},{2,0},{1,3},{3,1},{4,6},{6,4},{5,7},{7,5},{8,10},{10,8},{9,1... | collective-permute-start | bytes 24584 | tf_op jit(solution)/shard_map/ppermute | solution.py:136
  20.2 0.4 collective-permute-done.2
  20.6 3.0 %collective-permute-start.3 = (f32[64,128]{1,0:T(8,128)S(1)}, f32[64,128]{1,0:T(8,128)S(1)}, u32[]{:S(2)}, u32[]{:S(2)}) collective-permute-start(f32[64,128]{1,0:T(8,128)S(1)} %add.14), channel_id=1, source_target_pairs={{0,16},{4,20},{8,24},{12,28},{16,0},{20,4},{24,8},{28,12},{1,17},{... | collective-permute-start | bytes 98312 | tf_op jit(solution)/shard_map/ppermute | solution.py:136
  23.6 0.0 copy-done.4
  23.6 0.0 copy-done.5
  23.7 0.0 collective-permute-done
  23.7 1.8 %collective-permute-done.3 = f32[64,128]{1,0:T(8,128)S(1)} collective-permute-done((f32[64,128]{1,0:T(8,128)S(1)}, f32[64,128]{1,0:T(8,128)S(1)}, u32[]{:S(2)}, u32[]{:S(2)}) %collective-permute-start.3) | collective-permute-done | bytes 32800 | tf_op jit(solution)/shard_map/ppermute | solution.py:136
  25.5 2.7 %shard_map.83 = bf16[256,768]{1,0:T(8,128)(2,1)S(1)} custom-call(f32[16,128]{1,0:T(8,128)S(1)} %add.12.sum_x_ref, f32[64,128]{1,0:T(8,128)S(1)} %add.15.sum_y_ref, bf16[128,128]{1,0:T(8,128)(2,1)S(1)} %get-tuple-element.16.key_x_ref, bf16[128,128]{1,0:T(8,128)(2,1)S(1)} %get-tuple-element.11.key_y_ref, bf16[16,64,768]{2,1,0:T(8,128)(2,1)S(1)} %get-tuple-element.10.value_ref), custom_call_target="tpu_custom_call" | custom-call | flops 1073741824 | bytes 4194304 | tf_op jit(solution)/shard_map/pallas_call | solution.py:175
  28.3 0.0 copy-start.2
  28.3 16.9 %all_to_all.10 = bf16[16,16,768]{2,1,0:T(8,128)(2,1)S(1)} all-to-all(bf16[16,16,768]{2,1,0:T(8,128)(2,1)S(1)} %bitcast.6), channel_id=1, replica_groups=mesh['row'=8,'col'=2,'zs'=2] {'row','col'}, dimensions={0} | all-to-all | bytes 786432 | tf_op jit(solution)/shard_map/all_to_all | solution.py:145
  45.1 0.1 reduce_sum.12
  45.2 13.2 %all_to_all.11 = bf16[16,16,768]{2,1,0:T(8,128)(2,1)S(1)} all-to-all(bf16[16,16,768]{2,1,0:T(8,128)(2,1)S(1)} %broadcast_in_dim.3), channel_id=1, replica_groups=mesh['row'=8,'col'=2,'zs'=2] {'row','col'}, dimensions={0} | all-to-all | bytes 786432 | tf_op jit(solution)/shard_map/all_to_all | solution.py:148
  58.5 0.0 copy-done.2
  58.5 6.3 %shard_map.84 = bf16[16,6,64,128]{3,2,1,0:T(8,128)(2,1)} custom-call(f32[16,128]{1,0:T(8,128)S(1)} %add.12.sum_x_ref, f32[64,128]{1,0:T(8,128)S(1)} %add.15.sum_y_ref, bf16[128,128]{1,0:T(8,128)(2,1)S(1)} %get-tuple-element.15.query_x_ref, bf16[128,128]{1,0:T(8,128)(2,1)S(1)} %get-tuple-element.12.query_y_ref, bf16[256,768]{1,0:T(8,128)(2,1)S(1)} %bitcast.5, ...), custom_call_target="tpu_custom_call" | custom-call | flops 1073741824 | bytes 4194304 | tf_op jit(solution)/shard_map/pallas_call | solution.py:182
  (6 shorter events, 0.1 us)
Async XLA Ops:
  0.8 1.4 %copy-start = (bf16[16,64,6,128]{3,1,2,0:T(8,128)(2,1)S(1)}, bf16[16,64,6,128]{3,1,2,0:T(8,128)(2,1)}, u32[]{:S(2)}) copy-start(bf16[16,64,6,128]{3,1,2,0:T(8,128)(2,1)} %param.8) | copy-start | bytes 4718596
  2.2 0.8 %copy-start.1 = (bf16[128,128]{1,0:T(8,128)(2,1)S(1)}, bf16[128,128]{1,0:T(8,128)(2,1)}, u32[]{:S(2)}) copy-start(bf16[128,128]{1,0:T(8,128)(2,1)} %weight_ref.2) | copy-start | bytes 98308
  3.0 0.7 %copy-start.3 = (f32[128]{0:T(128)S(1)}, f32[128]{0:T(128)}, u32[]{:S(2)}) copy-start(f32[128]{0:T(128)} %param.9) | copy-start | bytes 1540
  3.6 20.0 %copy-start.4 = (bf16[128,256]{1,0:T(8,128)(2,1)S(1)}, bf16[128,256]{1,0:T(8,128)(2,1)}, u32[]{:S(2)}) copy-start(bf16[128,256]{1,0:T(8,128)(2,1)} %param.13) | copy-start | bytes 196612
  3.6 20.0 %copy-start.5 = (bf16[128,256]{1,0:T(8,128)(2,1)S(1)}, bf16[128,256]{1,0:T(8,128)(2,1)}, u32[]{:S(2)}) copy-start(bf16[128,256]{1,0:T(8,128)(2,1)} %param.11) | copy-start | bytes 196612
  11.7 4.9 %collective-permute-start.1 = (f32[64,128]{1,0:T(8,128)S(1)}, f32[64,128]{1,0:T(8,128)S(1)}, u32[]{:S(2)}, u32[]{:S(2)}) collective-permute-start(f32[64,128]{1,0:T(8,128)S(1)} %get-tuple-element.9), channel_id=1, source_target_pairs={{0,4},{4,0},{8,12},{12,8},{16,20},{20,16},{24,28},{28,24},{1,5},{5... | collective-permute-start | bytes 98312 | tf_op jit(solution)/shard_map/ppermute | solution.py:136
  16.6 4.0 %collective-permute-start.2 = (f32[64,128]{1,0:T(8,128)S(1)}, f32[64,128]{1,0:T(8,128)S(1)}, u32[]{:S(2)}, u32[]{:S(2)}) collective-permute-start(f32[64,128]{1,0:T(8,128)S(1)} %add.13), channel_id=1, source_target_pairs={{0,8},{4,12},{8,0},{12,4},{16,24},{20,28},{24,16},{28,20},{1,9},{5... | collective-permute-start | bytes 98312 | tf_op jit(solution)/shard_map/ppermute | solution.py:136
  18.7 5.0 %collective-permute-start = (f32[16,128]{1,0:T(8,128)S(1)}, f32[16,128]{1,0:T(8,128)S(1)}, u32[]{:S(2)}, u32[]{:S(2)}) collective-permute-start(f32[16,128]{1,0:T(8,128)S(1)} %get-tuple-element.8), channel_id=1, source_target_pairs={{0,2},{2,0},{1,3},{3,1},{4,6},{6,4},{5,7},{7,5},{8,10},{10,8},{9,1... | collective-permute-start | bytes 24584 | tf_op jit(solution)/shard_map/ppermute | solution.py:136
  20.6 4.9 %collective-permute-start.3 = (f32[64,128]{1,0:T(8,128)S(1)}, f32[64,128]{1,0:T(8,128)S(1)}, u32[]{:S(2)}, u32[]{:S(2)}) collective-permute-start(f32[64,128]{1,0:T(8,128)S(1)} %add.14), channel_id=1, source_target_pairs={{0,16},{4,20},{8,24},{12,28},{16,0},{20,4},{24,8},{28,12},{1,17},{... | collective-permute-start | bytes 98312 | tf_op jit(solution)/shard_map/ppermute | solution.py:136
  28.3 30.2 %copy-start.2 = (bf16[128,128]{1,0:T(8,128)(2,1)S(1)}, bf16[128,128]{1,0:T(8,128)(2,1)}, u32[]{:S(2)}) copy-start(bf16[128,128]{1,0:T(8,128)(2,1)} %weight_ref.3) | copy-start | bytes 98308

commit v2 on v1

v2 whole, which is shorter than its diff:
```python
import functools

import jax
import jax.numpy as jnp
from jax import lax
from jax.experimental import pallas as pl
from jax.experimental.pallas import tpu as pltpu
from jax.sharding import PartitionSpec as P

H = 8
EPS = 1e-05
HIGH = lax.Precision.HIGHEST
F32 = jnp.float32
BF16 = jnp.bfloat16
GELU_A = 0.7978845608028654
GELU_B = GELU_A * 0.044715
VMEM_LIMIT = 48 * 1024 * 1024
CHUNKS = 4
CUTS = (0, 4, 8, 12, 16)
GROUP = 8
LIMIT_A = 62 * 1024 * 1024
IN_HBM = pl.BlockSpec(memory_space=pltpu.HBM)


def dot(a, b):
    return jnp.dot(a, b, preferred_element_type=F32)


def halves(a):
    high = a.astype(BF16)
    return high, (a - high.astype(F32)).astype(BF16)


def summary(sums, scale, second):
    return jnp.dot(sums * scale, second.astype(F32), precision=HIGH)


def spread_into(ref, rows):
    width = rows.shape[1]
    depth = width // H
    start = lax.broadcasted_iota(jnp.int32, rows.shape, 1) // depth * depth
    for d in range(depth):
        ref[:, d * width : (d + 1) * width] = jnp.take_along_axis(rows, start + d, axis=1)


def gelu_twice(h):
    return h + h * jnp.tanh(h * (GELU_A + GELU_B * (h * h)))


def norm_kernel(field_hbm, gain_hbm, first_hbm, sum_y_ref, normed_hbm, field_ref, normed_ref, gain_ref, first_ref, sems):
    x_local, z_local, y_local, width = normed_ref.shape
    cuts = [x_local * k // 16 for k in CUTS]
    parts = [(a, b - a) for a, b in zip(cuts[:-1], cuts[1:])]
    count = len(parts)
    small = [
        pltpu.make_async_copy(gain_hbm, gain_ref, sems.at[2 * count]),
        pltpu.make_async_copy(first_hbm, first_ref, sems.at[2 * count + 1]),
    ]
    big = [
        pltpu.make_async_copy(field_hbm.at[pl.ds(a, n)], field_ref.at[pl.ds(a, n)], sems.at[c])
        for c, (a, n) in enumerate(parts)
    ]
    for copy in small + big:
        copy.start()
    for copy in small:
        copy.wait()
    gain = gain_ref[...]
    sum_y_ref[...] = jnp.zeros_like(sum_y_ref)
    outs = []

    for c, (a, n) in enumerate(parts):
        big[c].wait()
        part = pl.ds(a, n)
        values = field_ref[part].reshape(n * z_local * y_local, width).astype(F32)
        centred = values - jnp.mean(values, axis=-1, keepdims=True)
        spread = jnp.mean(centred * centred, axis=-1, keepdims=True)
        normed = (centred * lax.rsqrt(spread + EPS) * gain).astype(BF16)
        normed_ref[part] = normed.reshape(n, z_local, y_local, width)
        out = pltpu.make_async_copy(normed_ref.at[part], normed_hbm.at[part], sems.at[count + c])
        out.start()
        outs.append(out)
        g = gelu_twice(dot(normed, first_ref[...]))
        sum_y_ref[...] += jnp.sum(g.reshape(n * z_local, y_local, width), axis=0)
    for out in outs:
        out.wait()


def chunks_of(hbm, ref, sems):
    n = ref.shape[0] // CHUNKS
    copies = [
        pltpu.make_async_copy(hbm.at[pl.ds(c * n, n)], ref.at[pl.ds(c * n, n)], sems.at[c]) for c in range(CHUNKS)
    ]
    for copy in copies:
        copy.start()
    for c in range(CHUNKS):
        copies[c].wait()
        yield c * n, ref[pl.ds(c * n, n)].reshape(-1, ref.shape[3]), n


def sum_x_kernel(normed_hbm, first_hbm, sum_x_ref, normed_ref, first_ref, sems):
    load = pltpu.make_async_copy(first_hbm, first_ref, sems.at[CHUNKS])
    load.start()
    for start, rows, n in chunks_of(normed_hbm, normed_ref, sems):
        if start == 0:
            load.wait()
        g = gelu_twice(dot(rows, first_ref[...]))
        sum_x_ref[start : start + n, :] = jnp.sum(g.reshape(n, -1, g.shape[1]), axis=1)


def value_kernel(normed_hbm, weight_hbm, value_ref, normed_ref, weight_ref, sems):
    z_local, y_local, width = normed_ref.shape[1:]
    load = pltpu.make_async_copy(weight_hbm, weight_ref, sems.at[CHUNKS])
    load.start()
    for start, rows, n in chunks_of(normed_hbm, normed_ref, sems):
        if start == 0:
            load.wait()
        value = dot(rows, weight_ref[...]).astype(BF16).reshape(n, z_local, y_local, width)
        for z in range(z_local):
            value_ref[start : start + n, :, z * width : (z + 1) * width] = value[:, z]


def outer_kernel(scale_x, scale_y, sum_x_ref, sum_y_ref, key_x_ref, key_y_ref, value_ref, total_ref, part_ref, rows_ref):
    x_local, y_local, lanes = value_ref.shape
    width = key_x_ref.shape[0]
    depth = width // H
    key_y = summary(sum_y_ref[...], scale_y, key_y_ref[...])
    left = jnp.concatenate(halves(key_y.T), axis=1)
    spread_into(rows_ref, summary(sum_x_ref[...], scale_x, key_x_ref[...]))
    head = (lax.broadcasted_iota(jnp.int32, (depth, lanes), 1) % width) // depth

    def step(j, carry):
        group = [j * GROUP + q for q in range(GROUP)]
        fulls = [dot(left, jnp.concatenate([value_ref[i]] * 2, axis=0)) for i in group]
        for i, full in zip(group, fulls):
            acc = full[:depth]
            for h in range(1, H):
                acc = jnp.where(head == h, full[h * depth : (h + 1) * depth], acc)
            part_ref[i] = acc
        return carry

    lax.fori_loop(0, x_local // GROUP, step, 0)

    for z in range(lanes // width):
        cols = slice(z * width, (z + 1) * width)
        for d in range(depth):
            acc = jnp.zeros((depth, width), F32)
            for i in range(x_local):
                acc += rows_ref[i : i + 1, d * width : (d + 1) * width] * part_ref[i, :, cols]
            total_ref[d * depth : (d + 1) * depth, cols] = acc.astype(BF16)


def finish_kernel(
    scale_x, scale_y, sum_x_ref, sum_y_ref, query_x_ref, query_y_ref, total_ref, weight_ref,
    out_hbm, out_ref, wide_ref, rows_ref, sems,
):
    x_local, z_local, y_local, width = out_ref.shape
    depth = width // H
    lanes = z_local * width
    wide_ref[...] = total_ref[...].astype(F32)
    query_y = summary(sum_y_ref[...], scale_y, query_y_ref[...])
    high, low = halves(query_y)
    left = jnp.concatenate(
        [jnp.concatenate([high, high], axis=1), jnp.concatenate([low, jnp.zeros_like(low)], axis=1)], axis=0
    )
    spread_into(rows_ref, summary(sum_x_ref[...], scale_x, query_x_ref[...]))
    head = (lax.broadcasted_iota(jnp.int32, (depth, lanes), 1) % width) // depth
    zero = jnp.zeros((depth, lanes), BF16)

    def copy_of(i):
        return pltpu.make_async_copy(out_ref.at[i], out_hbm.at[i], sems.at[i])

    def right_of(i):
        pieces = []
        rows = rows_ref[pl.ds(i, 1), :]
        for z in range(z_local):
            cols = slice(z * width, (z + 1) * width)
            acc = jnp.zeros((depth, width), F32)
            for d in range(depth):
                acc += rows[:, d * width : (d + 1) * width] * wide_ref[d * depth : (d + 1) * depth, cols]
            pieces.append(acc)
        return jnp.concatenate(
            [jnp.where(head == h, w, zero) for w in halves(jnp.concatenate(pieces, axis=1)) for h in range(H)],
            axis=0,
        )

    def step(j, carry):
        group = [j * GROUP + q for q in range(GROUP)]
        boths = [dot(left, right) for right in [right_of(i) for i in group]]
        for i, both in zip(group, boths):
            u = (both[:y_local] + both[y_local:]).astype(BF16)
            u = jnp.concatenate([u[:, z * width : (z + 1) * width] for z in range(z_local)], axis=0)
            out_ref[i] = dot(u, weight_ref[...]).astype(BF16).reshape(z_local, y_local, width)
            copy_of(i).start()
        return carry

    lax.fori_loop(0, x_local // GROUP, step, 0)

    def finish(i, carry):
        copy_of(i).wait()
        return carry

    lax.fori_loop(0, x_local, finish, 0)


def call(kernel, out_shape, flops, scratch=(), limit=VMEM_LIMIT, **specs):
    return pl.pallas_call(
        kernel,
        out_shape=out_shape,
        scratch_shapes=list(scratch),
        compiler_params=pltpu.CompilerParams(vmem_limit_bytes=limit),
        cost_estimate=pl.CostEstimate(flops=flops, bytes_accessed=4 << 20, transcendentals=0),
        **specs,
    )


def exchange(value, axis, bit):
    return value + lax.ppermute(value, axis, [(i, i ^ bit) for i in range(lax.axis_size(axis))])


def pair_sums(sum_x, sum_y):
    sum_y = exchange(sum_y, "row", 1)
    sum_x, sum_y = lax.optimization_barrier((sum_x, sum_y))
    bit = 2
    while bit < lax.axis_size("row"):
        sum_y = exchange(sum_y, "row", bit)
        bit *= 2
    bit = 1
    while bit < lax.axis_size("col"):
        sum_x = exchange(sum_x, "col", bit)
        bit *= 2
    return sum_x, sum_y


def total_sum(part):
    axes = ("row", "col")
    n = lax.axis_size("row") * lax.axis_size("col")
    rows, lanes = part.shape
    blocks = lax.all_to_all(part.reshape(n, rows // n, lanes), axes, 0, 0)
    mine = jnp.sum(blocks.astype(F32), axis=0).astype(BF16)
    spread = jnp.broadcast_to(mine, blocks.shape)
    return lax.all_to_all(spread, axes, 0, 0).reshape(rows, lanes)


def body(field, norm_gain, first_x, second_x, first_y, second_y, value_weight, out_weight):
    x_local, y_local, z_local, width = field.shape
    depth = width // H
    lanes = z_local * width
    total_x = x_local * lax.axis_size("row")
    total_y = y_local * lax.axis_size("col")
    slab_shape = (x_local, z_local, y_local, width)
    sum_y, normed = call(
        norm_kernel,
        [jax.ShapeDtypeStruct((y_local, width), F32), jax.ShapeDtypeStruct(slab_shape, BF16)],
        1 << 30,
        [
            pltpu.VMEM(slab_shape, BF16),
            pltpu.VMEM(slab_shape, BF16),
            pltpu.VMEM((1, width), F32),
            pltpu.VMEM((width, width), BF16),
            pltpu.SemaphoreType.DMA((2 * len(CUTS),)),
        ],
        out_specs=[pl.BlockSpec(memory_space=pltpu.VMEM), IN_HBM],
        limit=LIMIT_A,
        in_specs=[IN_HBM] * 3,
    )(jnp.transpose(field, (0, 2, 1, 3)), norm_gain.reshape(1, width), first_y)
    loaded = [
        pltpu.VMEM(slab_shape, BF16),
        pltpu.VMEM((width, width), BF16),
        pltpu.SemaphoreType.DMA((CHUNKS + 1,)),
    ]
    sum_x = call(
        sum_x_kernel, jax.ShapeDtypeStruct((x_local, width), F32), 1 << 30, loaded, limit=LIMIT_A, in_specs=[IN_HBM] * 2
    )(normed, first_x)
    value = call(
        value_kernel, jax.ShapeDtypeStruct((x_local, y_local, lanes), BF16), 1 << 30, loaded, in_specs=[IN_HBM] * 2
    )(normed, value_weight)
    sum_x, sum_y = pair_sums(sum_x, sum_y)
    mean_x = 0.5 / (total_y * z_local)
    mean_y = 0.5 / (total_x * z_local)
    part = call(
        functools.partial(outer_kernel, mean_x, mean_y),
        jax.ShapeDtypeStruct((depth * depth, lanes), BF16),
        1 << 30,
        [pltpu.VMEM((x_local, depth, lanes), F32), pltpu.VMEM((x_local, depth * width), F32)],
    )(sum_x, sum_y, second_x[:, width:], second_y[:, width:], value)
    total = total_sum(part)
    out = call(
        functools.partial(finish_kernel, mean_x * total_x**-0.5, mean_y * total_y**-0.5),
        jax.ShapeDtypeStruct(slab_shape, BF16),
        1 << 30,
        [
            pltpu.VMEM(slab_shape, BF16),
            pltpu.VMEM((depth * depth, lanes), F32),
            pltpu.VMEM((x_local, depth * width), F32),
            pltpu.SemaphoreType.DMA((x_local,)),
        ],
        out_specs=IN_HBM,
    )(sum_x, sum_y, second_x[:, :width], second_y[:, :width], total, out_weight)
    return jnp.transpose(out, (0, 2, 1, 3))


def solution(mesh):
    placed = (P("row", "col", "zs", None), P(), P(), P(), P(), P(), P(), P())
    return jax.shard_map(
        body, mesh=mesh, in_specs=placed, out_specs=P("row", "col", "zs", None), check_vma=False
    )
```

time: 65.2 us -> 55.7 us (0.85)
  waiting for transfers between devices: 4.1 us -> 0.73 us
  local copies, waits for them, and re-layouts: 2.88 us -> 0.08 us
  blocking collectives: 30.1 us -> 29 us
  other arithmetic: 0.86 us -> 0.08 us
  starting transfers between devices: 9.66 us -> 8.88 us
    ppermute x4, waiting for transfers between devices: 4.1 us -> 0.73 us  [exchange(): lax.ppermute(value, axis, [(i, i ^ bit) for i in range(lax.axis_size(axis...]
    unnamed x12 -> x14, local copies, waits for them, and re-layouts: 2.83 us -> 0.03 us
    pallas_call x1, Pallas kernels: 6.28 us -> 3.52 us  [body(): call(functools.partial(finish_kernel, mean_x * total_x ** (-0.5), mean_y...]
    pallas_call x1 -> x3, Pallas kernels: 8.07 us -> 10.7 us  [the longest x1 5.16 us: body(): call(norm_kernel, [jax.ShapeDtypeStruct((y_local, width), F32), jax.Shape...]
    all_to_all x1, blocking collectives: 16.9 us -> 15.8 us  [total_sum(): blocks = lax.all_to_all(part.reshape(n, rows // n, lanes), axes, 0, 0)]
    concatenate x1 -> x0, other arithmetic: 0.78 us -> none  [body(): jnp.concatenate([first_x, first_y], axis=1)]
    ppermute x4, starting transfers between devices: 9.66 us -> 8.88 us  [exchange(): lax.ppermute(value, axis, [(i, i ^ bit) for i in range(lax.axis_size(axis...]
  transfers between devices with their start and end apart: 4 -> 4, of which waited for: 3 -> 1; matrix products, arithmetic and copies ran while one was open for 0% -> 0% of each run, Pallas kernels for 0% -> 10%
where the time goes in v2:
time: 55.7 us; the launch traced here: 55.5 us
  blocking collectives  29 us (52%)
  Pallas kernels  16.6 us (30%)
  starting transfers between devices  8.88 us (16%)
  waiting for transfers between devices  0.73 us (1%)
    all_to_all x1, blocking collectives, total_sum(): blocks = lax.all_to_all(part.reshape(n, rows // n, lanes), axes, 0, 0)  15.8 us
    all_to_all x1, blocking collectives, total_sum(): return lax.all_to_all(spread, axes, 0, 0).reshape(rows, lanes)  13.2 us
    ppermute x4, starting transfers between devices, exchange(): lax.ppermute(value, axis, [(i, i ^ bit) for i in range(lax.axis_size(axis...  8.88 us
    pallas_call x1, Pallas kernels, body(): call(norm_kernel, [jax.ShapeDtypeStruct((y_local, width), F32), jax.Shape...  5.16 us
    pallas_call x1, Pallas kernels, body(): call(functools.partial(finish_kernel, mean_x * total_x ** (-0.5), mean_y...  3.52 us
    pallas_call x1, Pallas kernels, body(): call(sum_x_kernel, jax.ShapeDtypeStruct((x_local, width), F32), 1 << 30,...  3.28 us
    pallas_call x1, Pallas kernels, body(): call(functools.partial(outer_kernel, mean_x, mean_y), jax.ShapeDtypeStruc...  2.38 us
    pallas_call x1, Pallas kernels, body(): call(value_kernel, jax.ShapeDtypeStruct((x_local, y_local, lanes), BF16),...  2.21 us
  transfers between devices with their start and end apart: 4, of which 1 were waited for; matrix products, arithmetic and copies ran while one was open for 0% of the time, Pallas kernels for 10%

profile of v2, /device:TPU:0, one launch (start us, length us, event | category | flops | bytes accessed | tf_op | source)
XLA Modules:
  0.0 55.5 jit_solution(4838838637611448652)
XLA Ops:
  0.0 5.2 %shard_map.82 = (f32[64,128]{1,0:T(8,128)}, bf16[16,6,64,128]{3,2,1,0:T(8,128)(2,1)}) custom-call(bf16[16,6,64,128]{3,2,1,0:T(8,128)(2,1)} %bitcast.7, f32[1,128]{1,0:T(1,128)} %bitcast.8, bf16[128,128]{1,0:T(8,128)(2,1)} %first_hbm.2), custom_call_target="tpu_custom_call" | custom-call | flops 1073741824 | bytes 4194304 | tf_op jit(solution)/shard_map/pallas_call | solution.py:251
  5.2 3.0 %collective-permute-start = (f32[64,128]{1,0:T(8,128)}, f32[64,128]{1,0:T(8,128)S(1)}, u32[]{:S(2)}, u32[]{:S(2)}) collective-permute-start(f32[64,128]{1,0:T(8,128)} %get-tuple-element.10), channel_id=1, source_target_pairs={{0,4},{4,0},{8,12},{12,8},{16,20},{20,16},{24,28},{28,24},{1,5},{5... | collective-permute-start | bytes 98312 | tf_op jit(solution)/shard_map/ppermute | solution.py:217
  8.2 0.0 copy-start.5
  8.2 0.0 copy-start.3
  8.2 0.0 copy-start.4
  8.2 0.0 copy-start
  8.2 0.0 copy-start.2
  8.2 3.3 %shard_map.83 = f32[16,128]{1,0:T(8,128)} custom-call(bf16[16,6,64,128]{3,2,1,0:T(8,128)(2,1)} %get-tuple-element.9.normed_hbm, bf16[128,128]{1,0:T(8,128)(2,1)} %first_hbm.3), custom_call_target="tpu_custom_call" | custom-call | flops 1073741824 | bytes 4194304 | tf_op jit(solution)/shard_map/pallas_call | solution.py:271
  11.5 0.0 collective-permute-done
  11.5 0.0 copy-done.5
  11.5 1.6 %collective-permute-start.2 = (f32[64,128]{1,0:T(8,128)S(1)}, f32[64,128]{1,0:T(8,128)S(1)}, u32[]{:S(2)}, u32[]{:S(2)}) collective-permute-start(f32[64,128]{1,0:T(8,128)S(1)} %add.12), channel_id=1, source_target_pairs={{0,8},{4,12},{8,0},{12,4},{16,24},{20,28},{24,16},{28,20},{1,9},{5... | collective-permute-start | bytes 98312 | tf_op jit(solution)/shard_map/ppermute | solution.py:217
  13.2 0.0 copy-done.3
  13.2 0.0 copy-done.4
  13.2 1.6 %collective-permute-start.1 = (f32[16,128]{1,0:T(8,128)}, f32[16,128]{1,0:T(8,128)S(1)}, u32[]{:S(2)}, u32[]{:S(2)}) collective-permute-start(f32[16,128]{1,0:T(8,128)} %shard_map.83), channel_id=1, source_target_pairs={{0,2},{2,0},{1,3},{3,1},{4,6},{6,4},{5,7},{7,5},{8,10},{10,8},{9,1... | collective-permute-start | bytes 24584 | tf_op jit(solution)/shard_map/ppermute | solution.py:217
  14.8 0.7 %collective-permute-done.2 = f32[64,128]{1,0:T(8,128)S(1)} collective-permute-done((f32[64,128]{1,0:T(8,128)S(1)}, f32[64,128]{1,0:T(8,128)S(1)}, u32[]{:S(2)}, u32[]{:S(2)}) %collective-permute-start.2) | collective-permute-done | bytes 32800 | tf_op jit(solution)/shard_map/ppermute | solution.py:217
  15.5 0.0 copy-start.6
  15.5 2.7 %collective-permute-start.3 = (f32[64,128]{1,0:T(8,128)S(1)}, f32[64,128]{1,0:T(8,128)S(1)}, u32[]{:S(2)}, u32[]{:S(2)}) collective-permute-start(f32[64,128]{1,0:T(8,128)S(1)} %add.14), channel_id=1, source_target_pairs={{0,16},{4,20},{8,24},{12,28},{16,0},{20,4},{24,8},{28,12},{1,17},{... | collective-permute-start | bytes 98312 | tf_op jit(solution)/shard_map/ppermute | solution.py:217
  18.2 0.0 copy-done
  18.2 0.0 copy-done.2
  18.2 2.2 %shard_map.84.value_ref = bf16[16,64,768]{2,1,0:T(8,128)(2,1)S(1)} custom-call(bf16[16,6,64,128]{3,2,1,0:T(8,128)(2,1)S(1)} %copy-done.2, bf16[128,128]{1,0:T(8,128)(2,1)S(1)} %copy-done), custom_call_target="tpu_custom_call" | custom-call | flops 1073741824 | bytes 4194304 | tf_op jit(solution)/shard_map/pallas_call | solution.py:274
  20.4 0.0 collective-permute-done.1
  20.4 0.0 copy-done.6
  20.4 0.0 collective-permute-done.3
  20.5 2.4 %shard_map.85 = bf16[256,768]{1,0:T(8,128)(2,1)S(1)} custom-call(f32[16,128]{1,0:T(8,128)S(1)} %add.13.sum_x_ref, f32[64,128]{1,0:T(8,128)S(1)} %add.15.sum_y_ref, bf16[128,128]{1,0:T(8,128)(2,1)S(1)} %get-tuple-element.18.key_x_ref, bf16[128,128]{1,0:T(8,128)(2,1)S(1)} %get-tuple-element.13.key_y_ref, bf16[16,64,768]{2,1,0:T(8,128)(2,1)S(1)} %shard_map.84.value_ref), custom_call_target="tpu_custom_call" | custom-call | flops 1073741824 | bytes 4194304 | tf_op jit(solution)/shard_map/pallas_call | solution.py:280
  22.8 0.0 copy-start.1
  22.8 15.8 %all_to_all.10 = bf16[16,16,768]{2,1,0:T(8,128)(2,1)S(1)} all-to-all(bf16[16,16,768]{2,1,0:T(8,128)(2,1)S(1)} %bitcast.6), channel_id=1, replica_groups=mesh['row'=8,'col'=2,'zs'=2] {'row','col'}, dimensions={0} | all-to-all | bytes 786432 | tf_op jit(solution)/shard_map/all_to_all | solution.py:238
  38.6 0.1 reduce_sum.12
  38.7 13.2 %all_to_all.11 = bf16[16,16,768]{2,1,0:T(8,128)(2,1)S(1)} all-to-all(bf16[16,16,768]{2,1,0:T(8,128)(2,1)S(1)} %broadcast_in_dim.3), channel_id=1, replica_groups=mesh['row'=8,'col'=2,'zs'=2] {'row','col'}, dimensions={0} | all-to-all | bytes 786432 | tf_op jit(solution)/shard_map/all_to_all | solution.py:241
  52.0 0.0 copy-done.1
  52.0 3.5 %shard_map.86 = bf16[16,6,64,128]{3,2,1,0:T(8,128)(2,1)} custom-call(f32[16,128]{1,0:T(8,128)S(1)} %add.13.sum_x_ref, f32[64,128]{1,0:T(8,128)S(1)} %add.15.sum_y_ref, bf16[128,128]{1,0:T(8,128)(2,1)S(1)} %get-tuple-element.17.query_x_ref, bf16[128,128]{1,0:T(8,128)(2,1)S(1)} %get-tuple-element.14.query_y_ref, bf16[256,768]{1,0:T(8,128)(2,1)S(1)} %bitcast.5, ...), custom_call_target="tpu_custom_call" | custom-call | flops 1073741824 | bytes 4194304 | tf_op jit(solution)/shard_map/pallas_call | solution.py:287
  (6 shorter events, 0.1 us)
Async XLA Ops:
  5.2 6.3 %collective-permute-start = (f32[64,128]{1,0:T(8,128)}, f32[64,128]{1,0:T(8,128)S(1)}, u32[]{:S(2)}, u32[]{:S(2)}) collective-permute-start(f32[64,128]{1,0:T(8,128)} %get-tuple-element.10), channel_id=1, source_target_pairs={{0,4},{4,0},{8,12},{12,8},{16,20},{20,16},{24,28},{28,24},{1,5},{5... | collective-permute-start | bytes 98312 | tf_op jit(solution)/shard_map/ppermute | solution.py:217
  8.2 3.3 %copy-start.5 = (f32[64,128]{1,0:T(8,128)S(1)}, f32[64,128]{1,0:T(8,128)}, u32[]{:S(2)}) copy-start(f32[64,128]{1,0:T(8,128)} %get-tuple-element.10) | copy-start | bytes 98308
  8.2 5.0 %copy-start.3 = (bf16[128,256]{1,0:T(8,128)(2,1)S(1)}, bf16[128,256]{1,0:T(8,128)(2,1)}, u32[]{:S(2)}) copy-start(bf16[128,256]{1,0:T(8,128)(2,1)} %param.13) | copy-start | bytes 196612
  8.2 5.0 %copy-start.4 = (bf16[128,256]{1,0:T(8,128)(2,1)S(1)}, bf16[128,256]{1,0:T(8,128)(2,1)}, u32[]{:S(2)}) copy-start(bf16[128,256]{1,0:T(8,128)(2,1)} %param.11) | copy-start | bytes 196612
  8.2 10.0 %copy-start = (bf16[128,128]{1,0:T(8,128)(2,1)S(1)}, bf16[128,128]{1,0:T(8,128)(2,1)}, u32[]{:S(2)}) copy-start(bf16[128,128]{1,0:T(8,128)(2,1)} %weight_hbm.1) | copy-start | bytes 98308
  8.2 10.0 %copy-start.2 = (bf16[16,6,64,128]{3,2,1,0:T(8,128)(2,1)S(1)}, bf16[16,6,64,128]{3,2,1,0:T(8,128)(2,1)}, u32[]{:S(2)}) copy-start(bf16[16,6,64,128]{3,2,1,0:T(8,128)(2,1)} %get-tuple-element.9.normed_hbm) | copy-start | bytes 4718596
  11.5 4.0 %collective-permute-start.2 = (f32[64,128]{1,0:T(8,128)S(1)}, f32[64,128]{1,0:T(8,128)S(1)}, u32[]{:S(2)}, u32[]{:S(2)}) collective-permute-start(f32[64,128]{1,0:T(8,128)S(1)} %add.12), channel_id=1, source_target_pairs={{0,8},{4,12},{8,0},{12,4},{16,24},{20,28},{24,16},{28,20},{1,9},{5... | collective-permute-start | bytes 98312 | tf_op jit(solution)/shard_map/ppermute | solution.py:217
  13.2 7.2 %collective-permute-start.1 = (f32[16,128]{1,0:T(8,128)}, f32[16,128]{1,0:T(8,128)S(1)}, u32[]{:S(2)}, u32[]{:S(2)}) collective-permute-start(f32[16,128]{1,0:T(8,128)} %shard_map.83), channel_id=1, source_target_pairs={{0,2},{2,0},{1,3},{3,1},{4,6},{6,4},{5,7},{7,5},{8,10},{10,8},{9,1... | collective-permute-start | bytes 24584 | tf_op jit(solution)/shard_map/ppermute | solution.py:217
  15.5 4.9 %copy-start.6 = (f32[16,128]{1,0:T(8,128)S(1)}, f32[16,128]{1,0:T(8,128)}, u32[]{:S(2)}) copy-start(f32[16,128]{1,0:T(8,128)} %shard_map.83) | copy-start | bytes 24580
  15.5 4.9 %collective-permute-start.3 = (f32[64,128]{1,0:T(8,128)S(1)}, f32[64,128]{1,0:T(8,128)S(1)}, u32[]{:S(2)}, u32[]{:S(2)}) collective-permute-start(f32[64,128]{1,0:T(8,128)S(1)} %add.14), channel_id=1, source_target_pairs={{0,16},{4,20},{8,24},{12,28},{16,0},{20,4},{24,8},{28,12},{1,17},{... | collective-permute-start | bytes 98312 | tf_op jit(solution)/shard_map/ppermute | solution.py:217
  22.8 29.1 %copy-start.1 = (bf16[128,128]{1,0:T(8,128)(2,1)S(1)}, bf16[128,128]{1,0:T(8,128)(2,1)}, u32[]{:S(2)}) copy-start(bf16[128,128]{1,0:T(8,128)(2,1)} %weight_ref.1) | copy-start | bytes 98308

commit v3 on v2

--- a/solution.py
+++ b/solution.py
@@ -16,7 +16,7 @@
 GELU_B = GELU_A * 0.044715
 VMEM_LIMIT = 48 * 1024 * 1024
 CHUNKS = 4
-CUTS = (0, 4, 8, 12, 16)
+CUTS = (0, 2, 8, 14, 16)
 GROUP = 8
 LIMIT_A = 62 * 1024 * 1024
 IN_HBM = pl.BlockSpec(memory_space=pltpu.HBM)
@@ -149,20 +149,20 @@
             total_ref[d * depth : (d + 1) * depth, cols] = acc.astype(BF16)
 
 
-def finish_kernel(
-    scale_x, scale_y, sum_x_ref, sum_y_ref, query_x_ref, query_y_ref, total_ref, weight_ref,
-    out_hbm, out_ref, wide_ref, rows_ref, sems,
-):
+def query_kernel(scale_x, scale_y, sum_x_ref, sum_y_ref, query_x_ref, query_y_ref, left_ref, rows_ref):
+    high, low = halves(summary(sum_y_ref[...], scale_y, query_y_ref[...]))
+    left_ref[...] = jnp.concatenate(
+        [jnp.concatenate([high, high], axis=1), jnp.concatenate([low, jnp.zeros_like(low)], axis=1)], axis=0
+    )
+    spread_into(rows_ref, summary(sum_x_ref[...], scale_x, query_x_ref[...]))
+
+
+def finish_kernel(left_ref, rows_ref, total_ref, weight_ref, out_hbm, out_ref, wide_ref, sems):
     x_local, z_local, y_local, width = out_ref.shape
     depth = width // H
     lanes = z_local * width
     wide_ref[...] = total_ref[...].astype(F32)
-    query_y = summary(sum_y_ref[...], scale_y, query_y_ref[...])
-    high, low = halves(query_y)
-    left = jnp.concatenate(
-        [jnp.concatenate([high, high], axis=1), jnp.concatenate([low, jnp.zeros_like(low)], axis=1)], axis=0
-    )
-    spread_into(rows_ref, summary(sum_x_ref[...], scale_x, query_x_ref[...]))
+    left = left_ref[...]
     head = (lax.broadcasted_iota(jnp.int32, (depth, lanes), 1) % width) // depth
     zero = jnp.zeros((depth, lanes), BF16)
 
@@ -213,32 +213,48 @@
     )
 
 
-def exchange(value, axis, bit):
-    return value + lax.ppermute(value, axis, [(i, i ^ bit) for i in range(lax.axis_size(axis))])
-
-
-def pair_sums(sum_x, sum_y):
-    sum_y = exchange(sum_y, "row", 1)
-    sum_x, sum_y = lax.optimization_barrier((sum_x, sum_y))
-    bit = 2
-    while bit < lax.axis_size("row"):
-        sum_y = exchange(sum_y, "row", bit)
-        bit *= 2
-    bit = 1
-    while bit < lax.axis_size("col"):
-        sum_x = exchange(sum_x, "col", bit)
-        bit *= 2
-    return sum_x, sum_y
-
-
-def total_sum(part):
+def sum_over(value, axis, stride, radix):
+    total = value
+    for k in range(1, radix):
+        pairs = []
+        for i in range(lax.axis_size(axis)):
+            digit = i // stride % radix
+            pairs.append((i, i + ((digit + k) % radix - digit) * stride))
+        total = total + lax.ppermute(value, axis, pairs)
+    return total
+
+
+def digits(size):
+    steps = []
+    while size > 1:
+        radix = 2 if size == 2 else 4
+        size //= radix
+        steps.append((size, radix))
+    return steps
+
+
+def sums_over(value, axis):
+    for step in digits(lax.axis_size(axis)):
+        value = sum_over(value, axis, *step)
+    return value
+
+
+def total_sum(part, beside, *args):
     axes = ("row", "col")
-    n = lax.axis_size("row") * lax.axis_size("col")
+    rows_n, cols_n = lax.axis_size("row"), lax.axis_size("col")
+    half = rows_n // 2
+    n = half * cols_n
+    groups = [[(k * half + r) * cols_n + c for r in range(half) for c in range(cols_n)] for k in range(2)]
     rows, lanes = part.shape
-    blocks = lax.all_to_all(part.reshape(n, rows // n, lanes), axes, 0, 0)
-    mine = jnp.sum(blocks.astype(F32), axis=0).astype(BF16)
+    blocks = lax.all_to_all(part.reshape(n, rows // n, lanes), axes, 0, 0, axis_index_groups=groups)
+    mine = jnp.sum(blocks.astype(F32), axis=0)
+    swap = [(r, (r + half) % rows_n) for r in range(rows_n)]
+    mine, args = lax.optimization_barrier((mine, args))
+    other = lax.ppermute(mine.astype(BF16), "row", swap)
+    done = beside(*args)
+    mine, done = lax.optimization_barrier(((mine + other.astype(F32)).astype(BF16), done))
     spread = jnp.broadcast_to(mine, blocks.shape)
-    return lax.all_to_all(spread, axes, 0, 0).reshape(rows, lanes)
+    return lax.all_to_all(spread, axes, 0, 0, axis_index_groups=groups).reshape(rows, lanes), done
 
 
 def body(field, norm_gain, first_x, second_x, first_y, second_y, value_weight, out_weight):
@@ -274,7 +290,8 @@
     value = call(
         value_kernel, jax.ShapeDtypeStruct((x_local, y_local, lanes), BF16), 1 << 30, loaded, in_specs=[IN_HBM] * 2
     )(normed, value_weight)
-    sum_x, sum_y = pair_sums(sum_x, sum_y)
+    sum_x = sums_over(sum_x, "col")
+    sum_y = sums_over(sum_y, "row")
     mean_x = 0.5 / (total_y * z_local)
     mean_y = 0.5 / (total_x * z_local)
     part = call(
@@ -283,19 +300,26 @@
         1 << 30,
         [pltpu.VMEM((x_local, depth, lanes), F32), pltpu.VMEM((x_local, depth * width), F32)],
     )(sum_x, sum_y, second_x[:, width:], second_y[:, width:], value)
-    total = total_sum(part)
+    queries = call(
+        functools.partial(query_kernel, mean_x * total_x**-0.5, mean_y * total_y**-0.5),
+        [
+            jax.ShapeDtypeStruct((2 * y_local, 2 * width), BF16),
+            jax.ShapeDtypeStruct((x_local, depth * width), F32),
+        ],
+        1 << 30,
+    )
+    total, (left, rows) = total_sum(part, queries, sum_x, sum_y, second_x[:, :width], second_y[:, :width])
     out = call(
-        functools.partial(finish_kernel, mean_x * total_x**-0.5, mean_y * total_y**-0.5),
+        finish_kernel,
         jax.ShapeDtypeStruct(slab_shape, BF16),
         1 << 30,
         [
             pltpu.VMEM(slab_shape, BF16),
             pltpu.VMEM((depth * depth, lanes), F32),
-            pltpu.VMEM((x_local, depth * width), F32),
             pltpu.SemaphoreType.DMA((x_local,)),
         ],
         out_specs=IN_HBM,
-    )(sum_x, sum_y, second_x[:, :width], second_y[:, :width], total, out_weight)
+    )(left, rows, total, out_weight)
     return jnp.transpose(out, (0, 2, 1, 3))
 
 

time: 55.7 us -> 53.5 us (0.961)
  blocking collectives: 29 us -> 21.9 us
  waiting for transfers between devices: 0.73 us -> 4.14 us
  starting transfers between devices: 8.88 us -> 10.5 us
    all_to_all x2, blocking collectives: 29 us -> 21.9 us  [the longest x1 12 us: total_sum(): lax.all_to_all(part.reshape(n, rows // n, lanes), axes, 0, 0, axis_index_...]
    ppermute x4 -> x6, waiting for transfers between devices: 0.73 us -> 4.14 us  [the longest x1 3.96 us: total_sum(): other = lax.ppermute(mine.astype(BF16), 'row', swap)]
    ppermute x4 -> x6, starting transfers between devices: 8.88 us -> 10.5 us  [the longest x5 9.26 us: sum_over(): total = total + lax.ppermute(value, axis, pairs)]
    pallas_call x1 -> x2, Pallas kernels: 3.52 us -> 3.49 us  [the longest x1 3.15 us: body(): call(finish_kernel, jax.ShapeDtypeStruct(slab_shape, BF16), 1 << 30, [plt...]
  transfers between devices with their start and end apart: 4 -> 6, of which waited for: 1 -> 2; matrix products, arithmetic and copies ran while one was open for 0% -> 0% of each run, Pallas kernels for 10% -> 11%
where the time goes in v3:
time: 53.5 us; the launch traced here: 53.3 us
  blocking collectives  21.9 us (41%)
  Pallas kernels  16.4 us (31%)
  starting transfers between devices  10.5 us (20%)
  waiting for transfers between devices  4.14 us (8%)
    all_to_all x1, blocking collectives, total_sum(): lax.all_to_all(part.reshape(n, rows // n, lanes), axes, 0, 0, axis_index_...  12 us
    all_to_all x1, blocking collectives, total_sum(): lax.all_to_all(spread, axes, 0, 0, axis_index_groups=groups)  9.89 us
    ppermute x5, starting transfers between devices, sum_over(): total = total + lax.ppermute(value, axis, pairs)  9.26 us
    pallas_call x1, Pallas kernels, body(): call(norm_kernel, [jax.ShapeDtypeStruct((y_local, width), F32), jax.Shape...  5.04 us
    ppermute x1, waiting for transfers between devices, total_sum(): other = lax.ppermute(mine.astype(BF16), 'row', swap)  3.96 us
    pallas_call x1, Pallas kernels, body(): call(sum_x_kernel, jax.ShapeDtypeStruct((x_local, width), F32), 1 << 30,...  3.27 us
    pallas_call x1, Pallas kernels, body(): call(finish_kernel, jax.ShapeDtypeStruct(slab_shape, BF16), 1 << 30, [plt...  3.15 us
    pallas_call x1, Pallas kernels, body(): call(functools.partial(outer_kernel, mean_x, mean_y), jax.ShapeDtypeStruc...  2.38 us
  transfers between devices with their start and end apart: 6, of which 2 were waited for; matrix products, arithmetic and copies ran while one was open for 0% of the time, Pallas kernels for 11%

profile of v3, /device:TPU:0, one launch (start us, length us, event | category | flops | bytes accessed | tf_op | source)
XLA Modules:
  0.0 53.3 jit_solution(12748148296681846088)
XLA Ops:
  0.0 5.0 %shard_map.82 = (f32[64,128]{1,0:T(8,128)}, bf16[16,6,64,128]{3,2,1,0:T(8,128)(2,1)}) custom-call(bf16[16,6,64,128]{3,2,1,0:T(8,128)(2,1)} %bitcast.7, f32[1,128]{1,0:T(1,128)} %bitcast.8, bf16[128,128]{1,0:T(8,128)(2,1)} %first_hbm.2), custom_call_target="tpu_custom_call" | custom-call | flops 1073741824 | bytes 4194304 | tf_op jit(solution)/shard_map/pallas_call | solution.py:267
  5.0 5.1 %collective-permute-start.3 = (f32[64,128]{1,0:T(8,128)}, f32[64,128]{1,0:T(8,128)S(1)}, u32[]{:S(2)}, u32[]{:S(2)}) collective-permute-start(f32[64,128]{1,0:T(8,128)} %get-tuple-element.18), channel_id=1, source_target_pairs={{0,24},{4,28},{8,0},{12,4},{16,8},{20,12},{24,16},{28,20},{1,25},{... | collective-permute-start | bytes 98312 | tf_op jit(solution)/shard_map/ppermute | solution.py:223
  10.2 0.0 collective-permute-start.2
  10.2 1.0 %collective-permute-start.1 = (f32[64,128]{1,0:T(8,128)}, f32[64,128]{1,0:T(8,128)S(1)}, u32[]{:S(2)}, u32[]{:S(2)}) collective-permute-start(f32[64,128]{1,0:T(8,128)} %get-tuple-element.18), channel_id=1, source_target_pairs={{0,8},{4,12},{8,16},{12,20},{16,24},{20,28},{24,0},{28,4},{1,9},{5... | collective-permute-start | bytes 98312 | tf_op jit(solution)/shard_map/ppermute | solution.py:223
  11.2 0.0 copy-start.3
  11.2 0.0 copy-start.4
  11.2 0.0 copy-start.5
  11.2 0.0 copy-start
  11.2 0.0 copy-start.2
  11.2 3.3 %shard_map.83 = f32[16,128]{1,0:T(8,128)} custom-call(bf16[16,6,64,128]{3,2,1,0:T(8,128)(2,1)} %get-tuple-element.17.normed_hbm, bf16[128,128]{1,0:T(8,128)(2,1)} %first_hbm.3), custom_call_target="tpu_custom_call" | custom-call | flops 1073741824 | bytes 4194304 | tf_op jit(solution)/shard_map/pallas_call | solution.py:287
  14.5 1.6 %collective-permute-start = (f32[16,128]{1,0:T(8,128)}, f32[16,128]{1,0:T(8,128)S(1)}, u32[]{:S(2)}, u32[]{:S(2)}) collective-permute-start(f32[16,128]{1,0:T(8,128)} %shard_map.83), channel_id=1, source_target_pairs={{0,2},{2,0},{1,3},{3,1},{4,6},{6,4},{5,7},{7,5},{8,10},{10,8},{9,1... | collective-permute-start | bytes 24584 | tf_op jit(solution)/shard_map/ppermute | solution.py:223
  16.1 0.0 copy-done.3
  16.1 0.0 copy-done.4
  16.1 0.0 collective-permute-done.3
  16.1 0.0 collective-permute-done.2
  16.1 0.0 collective-permute-done.1
  16.1 0.0 copy-done.5
  16.1 0.0 copy-start.6
  16.2 1.6 %collective-permute-start.4 = (f32[64,128]{1,0:T(8,128)S(1)}, f32[64,128]{1,0:T(8,128)S(1)}, u32[]{:S(2)}, u32[]{:S(2)}) collective-permute-start(f32[64,128]{1,0:T(8,128)S(1)} %add_add_fusion), channel_id=1, source_target_pairs={{0,4},{4,0},{8,12},{12,8},{16,20},{20,16},{24,28},{28,24},{1,5},{5... | collective-permute-start | bytes 98312 | tf_op jit(solution)/shard_map/ppermute | solution.py:223
  17.7 0.0 copy-done
  17.7 0.0 copy-done.2
  17.7 2.2 %shard_map.84.value_ref = bf16[16,64,768]{2,1,0:T(8,128)(2,1)S(1)} custom-call(bf16[16,6,64,128]{3,2,1,0:T(8,128)(2,1)S(1)} %copy-done.2, bf16[128,128]{1,0:T(8,128)(2,1)S(1)} %copy-done), custom_call_target="tpu_custom_call" | custom-call | flops 1073741824 | bytes 4194304 | tf_op jit(solution)/shard_map/pallas_call | solution.py:290
  19.9 0.0 collective-permute-done
  20.0 0.0 copy-done.6
  20.0 0.2 collective-permute-done.4
  20.1 2.4 %shard_map.85 = bf16[256,768]{1,0:T(8,128)(2,1)S(1)} custom-call(f32[16,128]{1,0:T(8,128)S(1)} %add.18.sum_x_ref, f32[64,128]{1,0:T(8,128)S(1)} %add.22.sum_y_ref, bf16[128,128]{1,0:T(8,128)(2,1)S(1)} %get-tuple-element.33.key_x_ref, bf16[128,128]{1,0:T(8,128)(2,1)S(1)} %get-tuple-element.30.key_y_ref, bf16[16,64,768]{2,1,0:T(8,128)(2,1)S(1)} %shard_map.84.value_ref), custom_call_target="tpu_custom_call" | custom-call | flops 1073741824 | bytes 4194304 | tf_op jit(solution)/shard_map/pallas_call | solution.py:297
  22.5 12.0 %all_to_all.10 = bf16[8,32,768]{2,1,0:T(8,128)(2,1)S(1)} all-to-all(bf16[8,32,768]{2,1,0:T(8,128)(2,1)S(1)} %bitcast.5), channel_id=1, replica_groups={{0,2,4,6,8,10,12,14},{16,18,20,22,24,26,28,30},{1,3,5,7,9,11,13,15},{17..., dimensions={0} | all-to-all | bytes 786432 | tf_op jit(solution)/shard_map/all_to_all | solution.py:249
  34.5 0.1 convert_reduce_fusion
  34.6 0.0 copy-start.1
  34.6 1.3 %collective-permute-start.5 = (bf16[32,768]{1,0:T(8,128)(2,1)S(1)}, bf16[32,768]{1,0:T(8,128)(2,1)S(1)}, u32[]{:S(2)}, u32[]{:S(2)}) collective-permute-start(bf16[32,768]{1,0:T(8,128)(2,1)S(1)} %convert_element_type.13), channel_id=1, source_target_pairs={{0,16},{4,20},{8,24},{12,28},{16,0},{20,4},{24,8},{28,12},{1,17},{... | collective-permute-start | bytes 147464 | tf_op jit(solution)/shard_map/ppermute | solution.py:253
  35.9 0.3 shard_map.86
  36.2 4.0 %collective-permute-done.5 = bf16[32,768]{1,0:T(8,128)(2,1)S(1)} collective-permute-done((bf16[32,768]{1,0:T(8,128)(2,1)S(1)}, bf16[32,768]{1,0:T(8,128)(2,1)S(1)}, u32[]{:S(2)}, u32[]{:S(2)}) %collective-permute-start.5) | collective-permute-done | bytes 49184 | tf_op jit(solution)/shard_map/ppermute | solution.py:253
  40.2 9.9 %all_to_all.11 = bf16[8,32,768]{2,1,0:T(8,128)(2,1)S(1)} all-to-all(bf16[8,32,768]{2,1,0:T(8,128)(2,1)S(1)} %broadcast_in_dim.3), channel_id=1, replica_groups={{0,2,4,6,8,10,12,14},{16,18,20,22,24,26,28,30},{1,3,5,7,9,11,13,15},{17..., dimensions={0} | all-to-all | bytes 786432 | tf_op jit(solution)/shard_map/all_to_all | solution.py:257
  50.1 0.0 copy-done.1
  50.1 3.2 %shard_map.87 = bf16[16,6,64,128]{3,2,1,0:T(8,128)(2,1)} custom-call(bf16[128,256]{1,0:T(8,128)(2,1)S(1)} %get-tuple-element.26.left_ref, f32[16,2048]{1,0:T(8,128)S(1)} %get-tuple-element.27.rows_ref, bf16[256,768]{1,0:T(8,128)(2,1)S(1)} %bitcast.6, bf16[128,128]{1,0:T(8,128)(2,1)S(1)} %copy-done.1), custom_call_target="tpu_custom_call" | custom-call | flops 1073741824 | bytes 4194304 | tf_op jit(solution)/shard_map/pallas_call | solution.py:312
  (7 shorter events, 0.1 us)
Async XLA Ops:
  5.0 11.0 %collective-permute-start.3 = (f32[64,128]{1,0:T(8,128)}, f32[64,128]{1,0:T(8,128)S(1)}, u32[]{:S(2)}, u32[]{:S(2)}) collective-permute-start(f32[64,128]{1,0:T(8,128)} %get-tuple-element.18), channel_id=1, source_target_pairs={{0,24},{4,28},{8,0},{12,4},{16,8},{20,12},{24,16},{28,20},{1,25},{... | collective-permute-start | bytes 98312 | tf_op jit(solution)/shard_map/ppermute | solution.py:223
  10.2 6.0 %collective-permute-start.2 = (f32[64,128]{1,0:T(8,128)}, f32[64,128]{1,0:T(8,128)S(1)}, u32[]{:S(2)}, u32[]{:S(2)}) collective-permute-start(f32[64,128]{1,0:T(8,128)} %get-tuple-element.18), channel_id=1, source_target_pairs={{0,16},{4,20},{8,24},{12,28},{16,0},{20,4},{24,8},{28,12},{1,17},{... | collective-permute-start | bytes 98312 | tf_op jit(solution)/shard_map/ppermute | solution.py:223
  10.2 6.0 %collective-permute-start.1 = (f32[64,128]{1,0:T(8,128)}, f32[64,128]{1,0:T(8,128)S(1)}, u32[]{:S(2)}, u32[]{:S(2)}) collective-permute-start(f32[64,128]{1,0:T(8,128)} %get-tuple-element.18), channel_id=1, source_target_pairs={{0,8},{4,12},{8,16},{12,20},{16,24},{20,28},{24,0},{28,4},{1,9},{5... | collective-permute-start | bytes 98312 | tf_op jit(solution)/shard_map/ppermute | solution.py:223
  11.2 4.9 %copy-start.3 = (bf16[128,256]{1,0:T(8,128)(2,1)S(1)}, bf16[128,256]{1,0:T(8,128)(2,1)}, u32[]{:S(2)}) copy-start(bf16[128,256]{1,0:T(8,128)(2,1)} %param.13) | copy-start | bytes 196612
  11.2 4.9 %copy-start.4 = (bf16[128,256]{1,0:T(8,128)(2,1)S(1)}, bf16[128,256]{1,0:T(8,128)(2,1)}, u32[]{:S(2)}) copy-start(bf16[128,256]{1,0:T(8,128)(2,1)} %param.11) | copy-start | bytes 196612
  11.2 5.0 %copy-start.5 = (f32[64,128]{1,0:T(8,128)S(1)}, f32[64,128]{1,0:T(8,128)}, u32[]{:S(2)}) copy-start(f32[64,128]{1,0:T(8,128)} %get-tuple-element.18) | copy-start | bytes 98308
  11.2 6.5 %copy-start = (bf16[128,128]{1,0:T(8,128)(2,1)S(1)}, bf16[128,128]{1,0:T(8,128)(2,1)}, u32[]{:S(2)}) copy-start(bf16[128,128]{1,0:T(8,128)(2,1)} %weight_hbm.1) | copy-start | bytes 98308
  11.2 6.5 %copy-start.2 = (bf16[16,6,64,128]{3,2,1,0:T(8,128)(2,1)S(1)}, bf16[16,6,64,128]{3,2,1,0:T(8,128)(2,1)}, u32[]{:S(2)}) copy-start(bf16[16,6,64,128]{3,2,1,0:T(8,128)(2,1)} %get-tuple-element.17.normed_hbm) | copy-start | bytes 4718596
  14.5 5.5 %collective-permute-start = (f32[16,128]{1,0:T(8,128)}, f32[16,128]{1,0:T(8,128)S(1)}, u32[]{:S(2)}, u32[]{:S(2)}) collective-permute-start(f32[16,128]{1,0:T(8,128)} %shard_map.83), channel_id=1, source_target_pairs={{0,2},{2,0},{1,3},{3,1},{4,6},{6,4},{5,7},{7,5},{8,10},{10,8},{9,1... | collective-permute-start | bytes 24584 | tf_op jit(solution)/shard_map/ppermute | solution.py:223
  16.1 3.8 %copy-start.6 = (f32[16,128]{1,0:T(8,128)S(1)}, f32[16,128]{1,0:T(8,128)}, u32[]{:S(2)}) copy-start(f32[16,128]{1,0:T(8,128)} %shard_map.83) | copy-start | bytes 24580
  16.2 4.0 %collective-permute-start.4 = (f32[64,128]{1,0:T(8,128)S(1)}, f32[64,128]{1,0:T(8,128)S(1)}, u32[]{:S(2)}, u32[]{:S(2)}) collective-permute-start(f32[64,128]{1,0:T(8,128)S(1)} %add_add_fusion), channel_id=1, source_target_pairs={{0,4},{4,0},{8,12},{12,8},{16,20},{20,16},{24,28},{28,24},{1,5},{5... | collective-permute-start | bytes 98312 | tf_op jit(solution)/shard_map/ppermute | solution.py:223
  34.6 15.5 %copy-start.1 = (bf16[128,128]{1,0:T(8,128)(2,1)S(1)}, bf16[128,128]{1,0:T(8,128)(2,1)}, u32[]{:S(2)}) copy-start(bf16[128,128]{1,0:T(8,128)(2,1)} %weight_ref.1) | copy-start | bytes 98308
  34.6 5.6 %collective-permute-start.5 = (bf16[32,768]{1,0:T(8,128)(2,1)S(1)}, bf16[32,768]{1,0:T(8,128)(2,1)S(1)}, u32[]{:S(2)}, u32[]{:S(2)}) collective-permute-start(bf16[32,768]{1,0:T(8,128)(2,1)S(1)} %convert_element_type.13), channel_id=1, source_target_pairs={{0,16},{4,20},{8,24},{12,28},{16,0},{20,4},{24,8},{28,12},{1,17},{... | collective-permute-start | bytes 147464 | tf_op jit(solution)/shard_map/ppermute | solution.py:253

commit v4 on v3

--- a/solution.py
+++ b/solution.py
@@ -60,12 +60,9 @@
         pltpu.make_async_copy(field_hbm.at[pl.ds(a, n)], field_ref.at[pl.ds(a, n)], sems.at[c])
         for c, (a, n) in enumerate(parts)
     ]
-    for copy in small + big:
+    for copy in big[:1] + small + big[1:]:
         copy.start()
-    for copy in small:
-        copy.wait()
-    gain = gain_ref[...]
-    sum_y_ref[...] = jnp.zeros_like(sum_y_ref)
+    total = jnp.zeros(sum_y_ref.shape, F32)
     outs = []
 
     for c, (a, n) in enumerate(parts):
@@ -74,46 +71,36 @@
         values = field_ref[part].reshape(n * z_local * y_local, width).astype(F32)
         centred = values - jnp.mean(values, axis=-1, keepdims=True)
         spread = jnp.mean(centred * centred, axis=-1, keepdims=True)
-        normed = (centred * lax.rsqrt(spread + EPS) * gain).astype(BF16)
+        if c == 0:
+            for copy in small:
+                copy.wait()
+        normed = (centred * lax.rsqrt(spread + EPS) * gain_ref[...]).astype(BF16)
         normed_ref[part] = normed.reshape(n, z_local, y_local, width)
         out = pltpu.make_async_copy(normed_ref.at[part], normed_hbm.at[part], sems.at[count + c])
         out.start()
         outs.append(out)
         g = gelu_twice(dot(normed, first_ref[...]))
-        sum_y_ref[...] += jnp.sum(g.reshape(n * z_local, y_local, width), axis=0)
+        total += jnp.sum(g.reshape(n * z_local, y_local, width), axis=0)
+    sum_y_ref[...] = total
     for out in outs:
         out.wait()
 
 
-def chunks_of(hbm, ref, sems):
+def chunks_of(ref):
     n = ref.shape[0] // CHUNKS
-    copies = [
-        pltpu.make_async_copy(hbm.at[pl.ds(c * n, n)], ref.at[pl.ds(c * n, n)], sems.at[c]) for c in range(CHUNKS)
-    ]
-    for copy in copies:
-        copy.start()
     for c in range(CHUNKS):
-        copies[c].wait()
         yield c * n, ref[pl.ds(c * n, n)].reshape(-1, ref.shape[3]), n
 
 
-def sum_x_kernel(normed_hbm, first_hbm, sum_x_ref, normed_ref, first_ref, sems):
-    load = pltpu.make_async_copy(first_hbm, first_ref, sems.at[CHUNKS])
-    load.start()
-    for start, rows, n in chunks_of(normed_hbm, normed_ref, sems):
-        if start == 0:
-            load.wait()
+def sum_x_kernel(normed_ref, first_ref, sum_x_ref):
+    for start, rows, n in chunks_of(normed_ref):
         g = gelu_twice(dot(rows, first_ref[...]))
         sum_x_ref[start : start + n, :] = jnp.sum(g.reshape(n, -1, g.shape[1]), axis=1)
 
 
-def value_kernel(normed_hbm, weight_hbm, value_ref, normed_ref, weight_ref, sems):
+def value_kernel(normed_ref, weight_ref, value_ref):
     z_local, y_local, width = normed_ref.shape[1:]
-    load = pltpu.make_async_copy(weight_hbm, weight_ref, sems.at[CHUNKS])
-    load.start()
-    for start, rows, n in chunks_of(normed_hbm, normed_ref, sems):
-        if start == 0:
-            load.wait()
+    for start, rows, n in chunks_of(normed_ref):
         value = dot(rows, weight_ref[...]).astype(BF16).reshape(n, z_local, y_local, width)
         for z in range(z_local):
             value_ref[start : start + n, :, z * width : (z + 1) * width] = value[:, z]
@@ -279,17 +266,8 @@
         limit=LIMIT_A,
         in_specs=[IN_HBM] * 3,
     )(jnp.transpose(field, (0, 2, 1, 3)), norm_gain.reshape(1, width), first_y)
-    loaded = [
-        pltpu.VMEM(slab_shape, BF16),
-        pltpu.VMEM((width, width), BF16),
-        pltpu.SemaphoreType.DMA((CHUNKS + 1,)),
-    ]
-    sum_x = call(
-        sum_x_kernel, jax.ShapeDtypeStruct((x_local, width), F32), 1 << 30, loaded, limit=LIMIT_A, in_specs=[IN_HBM] * 2
-    )(normed, first_x)
-    value = call(
-        value_kernel, jax.ShapeDtypeStruct((x_local, y_local, lanes), BF16), 1 << 30, loaded, in_specs=[IN_HBM] * 2
-    )(normed, value_weight)
+    sum_x = call(sum_x_kernel, jax.ShapeDtypeStruct((x_local, width), F32), 1 << 30)(normed, first_x)
+    value = call(value_kernel, jax.ShapeDtypeStruct((x_local, y_local, lanes), BF16), 1 << 30)(normed, value_weight)
     sum_x = sums_over(sum_x, "col")
     sum_y = sums_over(sum_y, "row")
     mean_x = 0.5 / (total_y * z_local)

time: 53.5 us -> 52.6 us (0.983)
  Pallas kernels: 16.4 us -> 12.5 us
  waiting for transfers between devices: 4.14 us -> 6.48 us
  local copies, waits for them, and re-layouts: 0.08 us -> 1.48 us
  blocking collectives: 21.9 us -> 21.1 us
    ppermute x5, waiting for transfers between devices: 0.18 us -> 2.69 us  [sum_over(): total = total + lax.ppermute(value, axis, pairs)]
    pallas_call x1, Pallas kernels: 3.27 us -> 1 us  [body(): call(sum_x_kernel, jax.ShapeDtypeStruct((x_local, width), F32), 1 << 30)]
    pallas_call x1, Pallas kernels: 2.21 us -> 0.55 us  [body(): call(value_kernel, jax.ShapeDtypeStruct((x_local, y_local, lanes), BF16),...]
    unnamed x14, local copies, waits for them, and re-layouts: 0.03 us -> 1.43 us
    all_to_all x1, blocking collectives: 12 us -> 11.2 us  [total_sum(): lax.all_to_all(part.reshape(n, rows // n, lanes), axes, 0, 0, axis_index_...]
  transfers between devices with their start and end apart: 6 -> 6, of which waited for: 2 -> 3; matrix products, arithmetic and copies ran while one was open for 0% -> 0% of each run, Pallas kernels for 11% -> 4%
where the time goes in v4:
time: 52.6 us; the launch traced here: 52.4 us
  blocking collectives  21.1 us (40%)
  Pallas kernels  12.5 us (24%)
  starting transfers between devices  10.7 us (20%)
  waiting for transfers between devices  6.48 us (12%)
  local copies, waits for them, and re-layouts  1.48 us (3%)
    all_to_all x1, blocking collectives, total_sum(): lax.all_to_all(part.reshape(n, rows // n, lanes), axes, 0, 0, axis_index_...  11.2 us
    all_to_all x1, blocking collectives, total_sum(): lax.all_to_all(spread, axes, 0, 0, axis_index_groups=groups)  9.89 us
    ppermute x5, starting transfers between devices, sum_over(): total = total + lax.ppermute(value, axis, pairs)  9.25 us
    pallas_call x1, Pallas kernels, body(): call(norm_kernel, [jax.ShapeDtypeStruct((y_local, width), F32), jax.Shape...  5.08 us
    ppermute x1, waiting for transfers between devices, total_sum(): other = lax.ppermute(mine.astype(BF16), 'row', swap)  3.79 us
    pallas_call x1, Pallas kernels, body(): call(finish_kernel, jax.ShapeDtypeStruct(slab_shape, BF16), 1 << 30, [plt...  3.13 us
    ppermute x5, waiting for transfers between devices, sum_over(): total = total + lax.ppermute(value, axis, pairs)  2.69 us
    pallas_call x1, Pallas kernels, body(): call(functools.partial(outer_kernel, mean_x, mean_y), jax.ShapeDtypeStruc...  2.38 us
  transfers between devices with their start and end apart: 6, of which 3 were waited for; matrix products, arithmetic and copies ran while one was open for 0% of the time, Pallas kernels for 4%

profile of v4, /device:TPU:0, one launch (start us, length us, event | category | flops | bytes accessed | tf_op | source)
XLA Modules:
  0.0 52.4 jit_solution(2993813345448484122)
XLA Ops:
  0.0 0.0 copy-start
  0.0 5.1 %shard_map.82 = (f32[64,128]{1,0:T(8,128)}, bf16[16,6,64,128]{3,2,1,0:T(8,128)(2,1)}) custom-call(bf16[16,6,64,128]{3,2,1,0:T(8,128)(2,1)} %bitcast.7, f32[1,128]{1,0:T(1,128)} %bitcast.8, bf16[128,128]{1,0:T(8,128)(2,1)} %first_hbm.1), custom_call_target="tpu_custom_call" | custom-call | flops 1073741824 | bytes 4194304 | tf_op jit(solution)/shard_map/pallas_call | solution.py:254
  5.1 5.1 %collective-permute-start.3 = (f32[64,128]{1,0:T(8,128)}, f32[64,128]{1,0:T(8,128)S(1)}, u32[]{:S(2)}, u32[]{:S(2)}) collective-permute-start(f32[64,128]{1,0:T(8,128)} %get-tuple-element.18), channel_id=1, source_target_pairs={{0,24},{4,28},{8,0},{12,4},{16,8},{20,12},{24,16},{28,20},{1,25},{... | collective-permute-start | bytes 98312 | tf_op jit(solution)/shard_map/ppermute | solution.py:210
  10.2 0.0 collective-permute-start.2
  10.2 1.0 %collective-permute-start.1 = (f32[64,128]{1,0:T(8,128)}, f32[64,128]{1,0:T(8,128)S(1)}, u32[]{:S(2)}, u32[]{:S(2)}) collective-permute-start(f32[64,128]{1,0:T(8,128)} %get-tuple-element.18), channel_id=1, source_target_pairs={{0,8},{4,12},{8,16},{12,20},{16,24},{20,28},{24,0},{28,4},{1,9},{5... | collective-permute-start | bytes 98312 | tf_op jit(solution)/shard_map/ppermute | solution.py:210
  11.2 0.0 copy-done
  11.2 0.0 copy-start.3
  11.2 1.4 %copy-done.3 = bf16[16,6,64,128]{3,2,1,0:T(8,128)(2,1)S(1)} copy-done((bf16[16,6,64,128]{3,2,1,0:T(8,128)(2,1)S(1)}, bf16[16,6,64,128]{3,2,1,0:T(8,128)(2,1)}, u32[]{:S(2)}) %copy-start.3) | copy-done | bytes 1572888
  12.6 0.0 copy-start.4
  12.6 0.0 copy-start.5
  12.6 0.0 copy-start.6
  12.6 0.0 copy-start.1
  12.6 1.0 %shard_map.83 = f32[16,128]{1,0:T(8,128)S(1)} custom-call(bf16[16,6,64,128]{3,2,1,0:T(8,128)(2,1)S(1)} %copy-done.3, bf16[128,128]{1,0:T(8,128)(2,1)S(1)} %copy-done), custom_call_target="tpu_custom_call" | custom-call | flops 1073741824 | bytes 4194304 | tf_op jit(solution)/shard_map/pallas_call | solution.py:269
  13.6 1.6 %collective-permute-start = (f32[16,128]{1,0:T(8,128)S(1)}, f32[16,128]{1,0:T(8,128)S(1)}, u32[]{:S(2)}, u32[]{:S(2)}) collective-permute-start(f32[16,128]{1,0:T(8,128)S(1)} %shard_map.83), channel_id=1, source_target_pairs={{0,2},{2,0},{1,3},{3,1},{4,6},{6,4},{5,7},{7,5},{8,10},{10,8},{9,1... | collective-permute-start | bytes 24584 | tf_op jit(solution)/shard_map/ppermute | solution.py:210
  15.2 0.0 copy-done.4
  15.2 0.0 copy-done.5
  15.3 0.0 collective-permute-done.3
  15.3 0.0 collective-permute-done.2
  15.3 0.8 %collective-permute-done.1 = f32[64,128]{1,0:T(8,128)S(1)} collective-permute-done((f32[64,128]{1,0:T(8,128)}, f32[64,128]{1,0:T(8,128)S(1)}, u32[]{:S(2)}, u32[]{:S(2)}) %collective-permute-start.1) | collective-permute-done | bytes 32800 | tf_op jit(solution)/shard_map/ppermute | solution.py:210
  16.1 0.0 copy-done.6
  16.1 1.6 %collective-permute-start.4 = (f32[64,128]{1,0:T(8,128)S(1)}, f32[64,128]{1,0:T(8,128)S(1)}, u32[]{:S(2)}, u32[]{:S(2)}) collective-permute-start(f32[64,128]{1,0:T(8,128)S(1)} %add_add_fusion), channel_id=1, source_target_pairs={{0,4},{4,0},{8,12},{12,8},{16,20},{20,16},{24,28},{28,24},{1,5},{5... | collective-permute-start | bytes 98312 | tf_op jit(solution)/shard_map/ppermute | solution.py:210
  17.7 0.0 copy-done.1
  17.7 0.5 %shard_map.84.value_ref = bf16[16,64,768]{2,1,0:T(8,128)(2,1)S(1)} custom-call(bf16[16,6,64,128]{3,2,1,0:T(8,128)(2,1)S(1)} %copy-done.3, bf16[128,128]{1,0:T(8,128)(2,1)S(1)} %copy-done.1), custom_call_target="tpu_custom_call" | custom-call | flops 1073741824 | bytes 4194304 | tf_op jit(solution)/shard_map/pallas_call | solution.py:270
  18.3 0.0 collective-permute-done
  18.3 1.8 %collective-permute-done.4 = f32[64,128]{1,0:T(8,128)S(1)} collective-permute-done((f32[64,128]{1,0:T(8,128)S(1)}, f32[64,128]{1,0:T(8,128)S(1)}, u32[]{:S(2)}, u32[]{:S(2)}) %collective-permute-start.4) | collective-permute-done | bytes 32800 | tf_op jit(solution)/shard_map/ppermute | solution.py:210
  20.1 2.4 %shard_map.85 = bf16[256,768]{1,0:T(8,128)(2,1)S(1)} custom-call(f32[16,128]{1,0:T(8,128)S(1)} %add.18.sum_x_ref, f32[64,128]{1,0:T(8,128)S(1)} %add.22.sum_y_ref, bf16[128,128]{1,0:T(8,128)(2,1)S(1)} %get-tuple-element.33.key_x_ref, bf16[128,128]{1,0:T(8,128)(2,1)S(1)} %get-tuple-element.30.key_y_ref, bf16[16,64,768]{2,1,0:T(8,128)(2,1)S(1)} %shard_map.84.value_ref), custom_call_target="tpu_custom_call" | custom-call | flops 1073741824 | bytes 4194304 | tf_op jit(solution)/shard_map/pallas_call | solution.py:275
  22.5 11.2 %all_to_all.10 = bf16[8,32,768]{2,1,0:T(8,128)(2,1)S(1)} all-to-all(bf16[8,32,768]{2,1,0:T(8,128)(2,1)S(1)} %bitcast.5), channel_id=1, replica_groups={{0,2,4,6,8,10,12,14},{16,18,20,22,24,26,28,30},{1,3,5,7,9,11,13,15},{17..., dimensions={0} | all-to-all | bytes 786432 | tf_op jit(solution)/shard_map/all_to_all | solution.py:236
  33.7 0.1 convert_reduce_fusion
  33.7 0.0 copy-start.2
  33.8 1.5 %collective-permute-start.5 = (bf16[32,768]{1,0:T(8,128)(2,1)S(1)}, bf16[32,768]{1,0:T(8,128)(2,1)S(1)}, u32[]{:S(2)}, u32[]{:S(2)}) collective-permute-start(bf16[32,768]{1,0:T(8,128)(2,1)S(1)} %convert_element_type.13), channel_id=1, source_target_pairs={{0,16},{4,20},{8,24},{12,28},{16,0},{20,4},{24,8},{28,12},{1,17},{... | collective-permute-start | bytes 147464 | tf_op jit(solution)/shard_map/ppermute | solution.py:240
  35.2 0.3 shard_map.86
  35.5 3.8 %collective-permute-done.5 = bf16[32,768]{1,0:T(8,128)(2,1)S(1)} collective-permute-done((bf16[32,768]{1,0:T(8,128)(2,1)S(1)}, bf16[32,768]{1,0:T(8,128)(2,1)S(1)}, u32[]{:S(2)}, u32[]{:S(2)}) %collective-permute-start.5) | collective-permute-done | bytes 49184 | tf_op jit(solution)/shard_map/ppermute | solution.py:240
  39.4 9.9 %all_to_all.11 = bf16[8,32,768]{2,1,0:T(8,128)(2,1)S(1)} all-to-all(bf16[8,32,768]{2,1,0:T(8,128)(2,1)S(1)} %broadcast_in_dim.3), channel_id=1, replica_groups={{0,2,4,6,8,10,12,14},{16,18,20,22,24,26,28,30},{1,3,5,7,9,11,13,15},{17..., dimensions={0} | all-to-all | bytes 786432 | tf_op jit(solution)/shard_map/all_to_all | solution.py:244
  49.3 0.0 copy-done.2
  49.3 3.1 %shard_map.87 = bf16[16,6,64,128]{3,2,1,0:T(8,128)(2,1)} custom-call(bf16[128,256]{1,0:T(8,128)(2,1)S(1)} %get-tuple-element.26.left_ref, f32[16,2048]{1,0:T(8,128)S(1)} %get-tuple-element.27.rows_ref, bf16[256,768]{1,0:T(8,128)(2,1)S(1)} %bitcast.6, bf16[128,128]{1,0:T(8,128)(2,1)S(1)} %copy-done.2), custom_call_target="tpu_custom_call" | custom-call | flops 1073741824 | bytes 4194304 | tf_op jit(solution)/shard_map/pallas_call | solution.py:290
  (7 shorter events, 0.1 us)
Async XLA Ops:
  0.0 11.2 %copy-start = (bf16[128,128]{1,0:T(8,128)(2,1)S(1)}, bf16[128,128]{1,0:T(8,128)(2,1)}, u32[]{:S(2)}) copy-start(bf16[128,128]{1,0:T(8,128)(2,1)} %first_ref.1) | copy-start | bytes 98308
  5.1 10.2 %collective-permute-start.3 = (f32[64,128]{1,0:T(8,128)}, f32[64,128]{1,0:T(8,128)S(1)}, u32[]{:S(2)}, u32[]{:S(2)}) collective-permute-start(f32[64,128]{1,0:T(8,128)} %get-tuple-element.18), channel_id=1, source_target_pairs={{0,24},{4,28},{8,0},{12,4},{16,8},{20,12},{24,16},{28,20},{1,25},{... | collective-permute-start | bytes 98312 | tf_op jit(solution)/shard_map/ppermute | solution.py:210
  10.2 5.1 %collective-permute-start.2 = (f32[64,128]{1,0:T(8,128)}, f32[64,128]{1,0:T(8,128)S(1)}, u32[]{:S(2)}, u32[]{:S(2)}) collective-permute-start(f32[64,128]{1,0:T(8,128)} %get-tuple-element.18), channel_id=1, source_target_pairs={{0,16},{4,20},{8,24},{12,28},{16,0},{20,4},{24,8},{28,12},{1,17},{... | collective-permute-start | bytes 98312 | tf_op jit(solution)/shard_map/ppermute | solution.py:210
  10.2 5.9 %collective-permute-start.1 = (f32[64,128]{1,0:T(8,128)}, f32[64,128]{1,0:T(8,128)S(1)}, u32[]{:S(2)}, u32[]{:S(2)}) collective-permute-start(f32[64,128]{1,0:T(8,128)} %get-tuple-element.18), channel_id=1, source_target_pairs={{0,8},{4,12},{8,16},{12,20},{16,24},{20,28},{24,0},{28,4},{1,9},{5... | collective-permute-start | bytes 98312 | tf_op jit(solution)/shard_map/ppermute | solution.py:210
  11.2 1.4 %copy-start.3 = (bf16[16,6,64,128]{3,2,1,0:T(8,128)(2,1)S(1)}, bf16[16,6,64,128]{3,2,1,0:T(8,128)(2,1)}, u32[]{:S(2)}) copy-start(bf16[16,6,64,128]{3,2,1,0:T(8,128)(2,1)} %get-tuple-element.17.normed_ref) | copy-start | bytes 4718596
  12.6 2.6 %copy-start.4 = (bf16[128,256]{1,0:T(8,128)(2,1)S(1)}, bf16[128,256]{1,0:T(8,128)(2,1)}, u32[]{:S(2)}) copy-start(bf16[128,256]{1,0:T(8,128)(2,1)} %param.13) | copy-start | bytes 196612
  12.6 2.6 %copy-start.5 = (bf16[128,256]{1,0:T(8,128)(2,1)S(1)}, bf16[128,256]{1,0:T(8,128)(2,1)}, u32[]{:S(2)}) copy-start(bf16[128,256]{1,0:T(8,128)(2,1)} %param.11) | copy-start | bytes 196612
  12.6 3.5 %copy-start.6 = (f32[64,128]{1,0:T(8,128)S(1)}, f32[64,128]{1,0:T(8,128)}, u32[]{:S(2)}) copy-start(f32[64,128]{1,0:T(8,128)} %get-tuple-element.18) | copy-start | bytes 98308
  12.6 5.1 %copy-start.1 = (bf16[128,128]{1,0:T(8,128)(2,1)S(1)}, bf16[128,128]{1,0:T(8,128)(2,1)}, u32[]{:S(2)}) copy-start(bf16[128,128]{1,0:T(8,128)(2,1)} %weight_ref.2) | copy-start | bytes 98308
  13.6 4.6 %collective-permute-start = (f32[16,128]{1,0:T(8,128)S(1)}, f32[16,128]{1,0:T(8,128)S(1)}, u32[]{:S(2)}, u32[]{:S(2)}) collective-permute-start(f32[16,128]{1,0:T(8,128)S(1)} %shard_map.83), channel_id=1, source_target_pairs={{0,2},{2,0},{1,3},{3,1},{4,6},{6,4},{5,7},{7,5},{8,10},{10,8},{9,1... | collective-permute-start | bytes 24584 | tf_op jit(solution)/shard_map/ppermute | solution.py:210
  16.1 4.0 %collective-permute-start.4 = (f32[64,128]{1,0:T(8,128)S(1)}, f32[64,128]{1,0:T(8,128)S(1)}, u32[]{:S(2)}, u32[]{:S(2)}) collective-permute-start(f32[64,128]{1,0:T(8,128)S(1)} %add_add_fusion), channel_id=1, source_target_pairs={{0,4},{4,0},{8,12},{12,8},{16,20},{20,16},{24,28},{28,24},{1,5},{5... | collective-permute-start | bytes 98312 | tf_op jit(solution)/shard_map/ppermute | solution.py:210
  33.7 15.5 %copy-start.2 = (bf16[128,128]{1,0:T(8,128)(2,1)S(1)}, bf16[128,128]{1,0:T(8,128)(2,1)}, u32[]{:S(2)}) copy-start(bf16[128,128]{1,0:T(8,128)(2,1)} %weight_ref.3) | copy-start | bytes 98308
  33.8 5.6 %collective-permute-start.5 = (bf16[32,768]{1,0:T(8,128)(2,1)S(1)}, bf16[32,768]{1,0:T(8,128)(2,1)S(1)}, u32[]{:S(2)}, u32[]{:S(2)}) collective-permute-start(bf16[32,768]{1,0:T(8,128)(2,1)S(1)} %convert_element_type.13), channel_id=1, source_target_pairs={{0,16},{4,20},{8,24},{12,28},{16,0},{20,4},{24,8},{28,12},{1,17},{... | collective-permute-start | bytes 147464 | tf_op jit(solution)/shard_map/ppermute | solution.py:240

commit v5 on v4

--- a/solution.py
+++ b/solution.py
@@ -9,7 +9,6 @@
 
 H = 8
 EPS = 1e-05
-HIGH = lax.Precision.HIGHEST
 F32 = jnp.float32
 BF16 = jnp.bfloat16
 GELU_A = 0.7978845608028654
@@ -32,7 +31,7 @@
 
 
 def summary(sums, scale, second):
-    return jnp.dot(sums * scale, second.astype(F32), precision=HIGH)
+    return dot(jnp.concatenate(halves(sums * scale), axis=1), jnp.concatenate([second, second], axis=0))
 
 
 def spread_into(ref, rows):
@@ -63,13 +62,14 @@
     for copy in big[:1] + small + big[1:]:
         copy.start()
     total = jnp.zeros(sum_y_ref.shape, F32)
+    ones = jnp.full((width, width), 1.0 / width, BF16)
     outs = []
 
     for c, (a, n) in enumerate(parts):
         big[c].wait()
         part = pl.ds(a, n)
-        values = field_ref[part].reshape(n * z_local * y_local, width).astype(F32)
-        centred = values - jnp.mean(values, axis=-1, keepdims=True)
+        values = field_ref[part].reshape(n * z_local * y_local, width)
+        centred = values.astype(F32) - dot(values, ones)
         spread = jnp.mean(centred * centred, axis=-1, keepdims=True)
         if c == 0:
             for copy in small:

time: 52.6 us -> 52.3 us (level)
  transfers between devices with their start and end apart: 6 -> 6, of which waited for: 3 -> 3; matrix products, arithmetic and copies ran while one was open for 0% -> 0% of each run, Pallas kernels for 4% -> 3%
where the time goes in v5:
time: 52.3 us; the launch traced here: 52.1 us
  blocking collectives  21.1 us (40%)
  Pallas kernels  12.1 us (23%)
  starting transfers between devices  10.7 us (20%)
  waiting for transfers between devices  6.54 us (13%)
  local copies, waits for them, and re-layouts  1.48 us (3%)
    all_to_all x1, blocking collectives, total_sum(): lax.all_to_all(part.reshape(n, rows // n, lanes), axes, 0, 0, axis_index_...  11.2 us
    all_to_all x1, blocking collectives, total_sum(): lax.all_to_all(spread, axes, 0, 0, axis_index_groups=groups)  9.89 us
    ppermute x5, starting transfers between devices, sum_over(): total = total + lax.ppermute(value, axis, pairs)  9.26 us
    pallas_call x1, Pallas kernels, body(): call(norm_kernel, [jax.ShapeDtypeStruct((y_local, width), F32), jax.Shape...  4.86 us
    ppermute x1, waiting for transfers between devices, total_sum(): other = lax.ppermute(mine.astype(BF16), 'row', swap)  3.86 us
    pallas_call x1, Pallas kernels, body(): call(finish_kernel, jax.ShapeDtypeStruct(slab_shape, BF16), 1 << 30, [plt...  3.13 us
    ppermute x5, waiting for transfers between devices, sum_over(): total = total + lax.ppermute(value, axis, pairs)  2.69 us
    pallas_call x1, Pallas kernels, body(): call(functools.partial(outer_kernel, mean_x, mean_y), jax.ShapeDtypeStruc...  2.3 us
  transfers between devices with their start and end apart: 6, of which 3 were waited for; matrix products, arithmetic and copies ran while one was open for 0% of the time, Pallas kernels for 3%

profile of v5, /device:TPU:0, one launch (start us, length us, event | category | flops | bytes accessed | tf_op | source)
XLA Modules:
  0.0 52.1 jit_solution(7420187390138897823)
XLA Ops:
  0.0 0.0 copy-start
  0.0 4.9 %shard_map.82 = (f32[64,128]{1,0:T(8,128)}, bf16[16,6,64,128]{3,2,1,0:T(8,128)(2,1)}) custom-call(bf16[16,6,64,128]{3,2,1,0:T(8,128)(2,1)} %bitcast.7, f32[1,128]{1,0:T(1,128)} %bitcast.8, bf16[128,128]{1,0:T(8,128)(2,1)} %first_hbm.1), custom_call_target="tpu_custom_call" | custom-call | flops 1073741824 | bytes 4194304 | tf_op jit(solution)/shard_map/pallas_call | solution.py:254
  4.9 5.1 %collective-permute-start.3 = (f32[64,128]{1,0:T(8,128)}, f32[64,128]{1,0:T(8,128)S(1)}, u32[]{:S(2)}, u32[]{:S(2)}) collective-permute-start(f32[64,128]{1,0:T(8,128)} %get-tuple-element.18), channel_id=1, source_target_pairs={{0,24},{4,28},{8,0},{12,4},{16,8},{20,12},{24,16},{28,20},{1,25},{... | collective-permute-start | bytes 98312 | tf_op jit(solution)/shard_map/ppermute | solution.py:210
  10.0 0.0 collective-permute-start.2
  10.0 1.0 %collective-permute-start.1 = (f32[64,128]{1,0:T(8,128)}, f32[64,128]{1,0:T(8,128)S(1)}, u32[]{:S(2)}, u32[]{:S(2)}) collective-permute-start(f32[64,128]{1,0:T(8,128)} %get-tuple-element.18), channel_id=1, source_target_pairs={{0,8},{4,12},{8,16},{12,20},{16,24},{20,28},{24,0},{28,4},{1,9},{5... | collective-permute-start | bytes 98312 | tf_op jit(solution)/shard_map/ppermute | solution.py:210
  11.0 0.0 copy-done
  11.0 0.0 copy-start.3
  11.0 1.4 %copy-done.3 = bf16[16,6,64,128]{3,2,1,0:T(8,128)(2,1)S(1)} copy-done((bf16[16,6,64,128]{3,2,1,0:T(8,128)(2,1)S(1)}, bf16[16,6,64,128]{3,2,1,0:T(8,128)(2,1)}, u32[]{:S(2)}) %copy-start.3) | copy-done | bytes 1572888
  12.4 0.0 copy-start.4
  12.4 0.0 copy-start.5
  12.4 0.0 copy-start.6
  12.4 0.0 copy-start.1
  12.4 1.0 %shard_map.83 = f32[16,128]{1,0:T(8,128)S(1)} custom-call(bf16[16,6,64,128]{3,2,1,0:T(8,128)(2,1)S(1)} %copy-done.3, bf16[128,128]{1,0:T(8,128)(2,1)S(1)} %copy-done), custom_call_target="tpu_custom_call" | custom-call | flops 1073741824 | bytes 4194304 | tf_op jit(solution)/shard_map/pallas_call | solution.py:269
  13.4 1.6 %collective-permute-start = (f32[16,128]{1,0:T(8,128)S(1)}, f32[16,128]{1,0:T(8,128)S(1)}, u32[]{:S(2)}, u32[]{:S(2)}) collective-permute-start(f32[16,128]{1,0:T(8,128)S(1)} %shard_map.83), channel_id=1, source_target_pairs={{0,2},{2,0},{1,3},{3,1},{4,6},{6,4},{5,7},{7,5},{8,10},{10,8},{9,1... | collective-permute-start | bytes 24584 | tf_op jit(solution)/shard_map/ppermute | solution.py:210
  15.0 0.0 copy-done.4
  15.0 0.0 copy-done.5
  15.0 0.0 collective-permute-done.3
  15.1 0.0 collective-permute-done.2
  15.1 0.8 %collective-permute-done.1 = f32[64,128]{1,0:T(8,128)S(1)} collective-permute-done((f32[64,128]{1,0:T(8,128)}, f32[64,128]{1,0:T(8,128)S(1)}, u32[]{:S(2)}, u32[]{:S(2)}) %collective-permute-start.1) | collective-permute-done | bytes 32800 | tf_op jit(solution)/shard_map/ppermute | solution.py:210
  15.9 0.0 copy-done.6
  15.9 1.6 %collective-permute-start.4 = (f32[64,128]{1,0:T(8,128)S(1)}, f32[64,128]{1,0:T(8,128)S(1)}, u32[]{:S(2)}, u32[]{:S(2)}) collective-permute-start(f32[64,128]{1,0:T(8,128)S(1)} %add_add_fusion), channel_id=1, source_target_pairs={{0,4},{4,0},{8,12},{12,8},{16,20},{20,16},{24,28},{28,24},{1,5},{5... | collective-permute-start | bytes 98312 | tf_op jit(solution)/shard_map/ppermute | solution.py:210
  17.5 0.0 copy-done.1
  17.5 0.5 %shard_map.84.value_ref = bf16[16,64,768]{2,1,0:T(8,128)(2,1)S(1)} custom-call(bf16[16,6,64,128]{3,2,1,0:T(8,128)(2,1)S(1)} %copy-done.3, bf16[128,128]{1,0:T(8,128)(2,1)S(1)} %copy-done.1), custom_call_target="tpu_custom_call" | custom-call | flops 1073741824 | bytes 4194304 | tf_op jit(solution)/shard_map/pallas_call | solution.py:270
  18.0 0.0 collective-permute-done
  18.1 1.8 %collective-permute-done.4 = f32[64,128]{1,0:T(8,128)S(1)} collective-permute-done((f32[64,128]{1,0:T(8,128)S(1)}, f32[64,128]{1,0:T(8,128)S(1)}, u32[]{:S(2)}, u32[]{:S(2)}) %collective-permute-start.4) | collective-permute-done | bytes 32800 | tf_op jit(solution)/shard_map/ppermute | solution.py:210
  19.9 2.3 %shard_map.85 = bf16[256,768]{1,0:T(8,128)(2,1)S(1)} custom-call(f32[16,128]{1,0:T(8,128)S(1)} %add.18.sum_x_ref, f32[64,128]{1,0:T(8,128)S(1)} %add.22.sum_y_ref, bf16[128,128]{1,0:T(8,128)(2,1)S(1)} %get-tuple-element.33.key_x_ref, bf16[128,128]{1,0:T(8,128)(2,1)S(1)} %get-tuple-element.30.key_y_ref, bf16[16,64,768]{2,1,0:T(8,128)(2,1)S(1)} %shard_map.84.value_ref), custom_call_target="tpu_custom_call" | custom-call | flops 1073741824 | bytes 4194304 | tf_op jit(solution)/shard_map/pallas_call | solution.py:275
  22.2 11.2 %all_to_all.10 = bf16[8,32,768]{2,1,0:T(8,128)(2,1)S(1)} all-to-all(bf16[8,32,768]{2,1,0:T(8,128)(2,1)S(1)} %bitcast.5), channel_id=1, replica_groups={{0,2,4,6,8,10,12,14},{16,18,20,22,24,26,28,30},{1,3,5,7,9,11,13,15},{17..., dimensions={0} | all-to-all | bytes 786432 | tf_op jit(solution)/shard_map/all_to_all | solution.py:236
  33.4 0.1 convert_reduce_fusion
  33.4 0.0 copy-start.2
  33.5 1.5 %collective-permute-start.5 = (bf16[32,768]{1,0:T(8,128)(2,1)S(1)}, bf16[32,768]{1,0:T(8,128)(2,1)S(1)}, u32[]{:S(2)}, u32[]{:S(2)}) collective-permute-start(bf16[32,768]{1,0:T(8,128)(2,1)S(1)} %convert_element_type.13), channel_id=1, source_target_pairs={{0,16},{4,20},{8,24},{12,28},{16,0},{20,4},{24,8},{28,12},{1,17},{... | collective-permute-start | bytes 147464 | tf_op jit(solution)/shard_map/ppermute | solution.py:240
  34.9 0.3 shard_map.86
  35.2 3.9 %collective-permute-done.5 = bf16[32,768]{1,0:T(8,128)(2,1)S(1)} collective-permute-done((bf16[32,768]{1,0:T(8,128)(2,1)S(1)}, bf16[32,768]{1,0:T(8,128)(2,1)S(1)}, u32[]{:S(2)}, u32[]{:S(2)}) %collective-permute-start.5) | collective-permute-done | bytes 49184 | tf_op jit(solution)/shard_map/ppermute | solution.py:240
  39.1 9.9 %all_to_all.11 = bf16[8,32,768]{2,1,0:T(8,128)(2,1)S(1)} all-to-all(bf16[8,32,768]{2,1,0:T(8,128)(2,1)S(1)} %broadcast_in_dim.3), channel_id=1, replica_groups={{0,2,4,6,8,10,12,14},{16,18,20,22,24,26,28,30},{1,3,5,7,9,11,13,15},{17..., dimensions={0} | all-to-all | bytes 786432 | tf_op jit(solution)/shard_map/all_to_all | solution.py:244
  49.0 0.0 copy-done.2
  49.0 3.1 %shard_map.87 = bf16[16,6,64,128]{3,2,1,0:T(8,128)(2,1)} custom-call(bf16[128,256]{1,0:T(8,128)(2,1)S(1)} %get-tuple-element.26.left_ref, f32[16,2048]{1,0:T(8,128)S(1)} %get-tuple-element.27.rows_ref, bf16[256,768]{1,0:T(8,128)(2,1)S(1)} %bitcast.6, bf16[128,128]{1,0:T(8,128)(2,1)S(1)} %copy-done.2), custom_call_target="tpu_custom_call" | custom-call | flops 1073741824 | bytes 4194304 | tf_op jit(solution)/shard_map/pallas_call | solution.py:290
  (7 shorter events, 0.1 us)
Async XLA Ops:
  0.0 11.0 %copy-start = (bf16[128,128]{1,0:T(8,128)(2,1)S(1)}, bf16[128,128]{1,0:T(8,128)(2,1)}, u32[]{:S(2)}) copy-start(bf16[128,128]{1,0:T(8,128)(2,1)} %first_ref.1) | copy-start | bytes 98308
  4.9 10.2 %collective-permute-start.3 = (f32[64,128]{1,0:T(8,128)}, f32[64,128]{1,0:T(8,128)S(1)}, u32[]{:S(2)}, u32[]{:S(2)}) collective-permute-start(f32[64,128]{1,0:T(8,128)} %get-tuple-element.18), channel_id=1, source_target_pairs={{0,24},{4,28},{8,0},{12,4},{16,8},{20,12},{24,16},{28,20},{1,25},{... | collective-permute-start | bytes 98312 | tf_op jit(solution)/shard_map/ppermute | solution.py:210
  10.0 5.1 %collective-permute-start.2 = (f32[64,128]{1,0:T(8,128)}, f32[64,128]{1,0:T(8,128)S(1)}, u32[]{:S(2)}, u32[]{:S(2)}) collective-permute-start(f32[64,128]{1,0:T(8,128)} %get-tuple-element.18), channel_id=1, source_target_pairs={{0,16},{4,20},{8,24},{12,28},{16,0},{20,4},{24,8},{28,12},{1,17},{... | collective-permute-start | bytes 98312 | tf_op jit(solution)/shard_map/ppermute | solution.py:210
  10.0 5.9 %collective-permute-start.1 = (f32[64,128]{1,0:T(8,128)}, f32[64,128]{1,0:T(8,128)S(1)}, u32[]{:S(2)}, u32[]{:S(2)}) collective-permute-start(f32[64,128]{1,0:T(8,128)} %get-tuple-element.18), channel_id=1, source_target_pairs={{0,8},{4,12},{8,16},{12,20},{16,24},{20,28},{24,0},{28,4},{1,9},{5... | collective-permute-start | bytes 98312 | tf_op jit(solution)/shard_map/ppermute | solution.py:210
  11.0 1.4 %copy-start.3 = (bf16[16,6,64,128]{3,2,1,0:T(8,128)(2,1)S(1)}, bf16[16,6,64,128]{3,2,1,0:T(8,128)(2,1)}, u32[]{:S(2)}) copy-start(bf16[16,6,64,128]{3,2,1,0:T(8,128)(2,1)} %get-tuple-element.17.normed_ref) | copy-start | bytes 4718596
  12.4 2.6 %copy-start.4 = (bf16[128,256]{1,0:T(8,128)(2,1)S(1)}, bf16[128,256]{1,0:T(8,128)(2,1)}, u32[]{:S(2)}) copy-start(bf16[128,256]{1,0:T(8,128)(2,1)} %param.13) | copy-start | bytes 196612
  12.4 2.6 %copy-start.5 = (bf16[128,256]{1,0:T(8,128)(2,1)S(1)}, bf16[128,256]{1,0:T(8,128)(2,1)}, u32[]{:S(2)}) copy-start(bf16[128,256]{1,0:T(8,128)(2,1)} %param.11) | copy-start | bytes 196612
  12.4 3.5 %copy-start.6 = (f32[64,128]{1,0:T(8,128)S(1)}, f32[64,128]{1,0:T(8,128)}, u32[]{:S(2)}) copy-start(f32[64,128]{1,0:T(8,128)} %get-tuple-element.18) | copy-start | bytes 98308
  12.4 5.1 %copy-start.1 = (bf16[128,128]{1,0:T(8,128)(2,1)S(1)}, bf16[128,128]{1,0:T(8,128)(2,1)}, u32[]{:S(2)}) copy-start(bf16[128,128]{1,0:T(8,128)(2,1)} %weight_ref.2) | copy-start | bytes 98308
  13.4 4.6 %collective-permute-start = (f32[16,128]{1,0:T(8,128)S(1)}, f32[16,128]{1,0:T(8,128)S(1)}, u32[]{:S(2)}, u32[]{:S(2)}) collective-permute-start(f32[16,128]{1,0:T(8,128)S(1)} %shard_map.83), channel_id=1, source_target_pairs={{0,2},{2,0},{1,3},{3,1},{4,6},{6,4},{5,7},{7,5},{8,10},{10,8},{9,1... | collective-permute-start | bytes 24584 | tf_op jit(solution)/shard_map/ppermute | solution.py:210
  15.9 4.0 %collective-permute-start.4 = (f32[64,128]{1,0:T(8,128)S(1)}, f32[64,128]{1,0:T(8,128)S(1)}, u32[]{:S(2)}, u32[]{:S(2)}) collective-permute-start(f32[64,128]{1,0:T(8,128)S(1)} %add_add_fusion), channel_id=1, source_target_pairs={{0,4},{4,0},{8,12},{12,8},{16,20},{20,16},{24,28},{28,24},{1,5},{5... | collective-permute-start | bytes 98312 | tf_op jit(solution)/shard_map/ppermute | solution.py:210
  33.4 15.5 %copy-start.2 = (bf16[128,128]{1,0:T(8,128)(2,1)S(1)}, bf16[128,128]{1,0:T(8,128)(2,1)}, u32[]{:S(2)}) copy-start(bf16[128,128]{1,0:T(8,128)(2,1)} %weight_ref.3) | copy-start | bytes 98308
  33.5 5.6 %collective-permute-start.5 = (bf16[32,768]{1,0:T(8,128)(2,1)S(1)}, bf16[32,768]{1,0:T(8,128)(2,1)S(1)}, u32[]{:S(2)}, u32[]{:S(2)}) collective-permute-start(bf16[32,768]{1,0:T(8,128)(2,1)S(1)} %convert_element_type.13), channel_id=1, source_target_pairs={{0,16},{4,20},{8,24},{12,28},{16,0},{20,4},{24,8},{28,12},{1,17},{... | collective-permute-start | bytes 147464 | tf_op jit(solution)/shard_map/ppermute | solution.py:240

commit v6 on v5

--- a/solution.py
+++ b/solution.py
@@ -17,6 +17,7 @@
 CHUNKS = 4
 CUTS = (0, 2, 8, 14, 16)
 GROUP = 8
+WIDE_GROUP = 16
 LIMIT_A = 62 * 1024 * 1024
 IN_HBM = pl.BlockSpec(memory_space=pltpu.HBM)
 
@@ -171,7 +172,7 @@
         )
 
     def step(j, carry):
-        group = [j * GROUP + q for q in range(GROUP)]
+        group = [j * WIDE_GROUP + q for q in range(WIDE_GROUP)]
         boths = [dot(left, right) for right in [right_of(i) for i in group]]
         for i, both in zip(group, boths):
             u = (both[:y_local] + both[y_local:]).astype(BF16)
@@ -180,7 +181,7 @@
             copy_of(i).start()
         return carry
 
-    lax.fori_loop(0, x_local // GROUP, step, 0)
+    lax.fori_loop(0, x_local // WIDE_GROUP, step, 0)
 
     def finish(i, carry):
         copy_of(i).wait()

time: 52.3 us -> 52.2 us (level)
  no operation moved by 1% of the time
where the time goes in v6:
time: 52.2 us; the launch traced here: 52 us
  blocking collectives  21.1 us (40%)
  Pallas kernels  11.9 us (23%)
  starting transfers between devices  10.7 us (20%)
  waiting for transfers between devices  6.54 us (13%)
  local copies, waits for them, and re-layouts  1.48 us (3%)
    all_to_all x1, blocking collectives, total_sum(): lax.all_to_all(part.reshape(n, rows // n, lanes), axes, 0, 0, axis_index_...  11.2 us
    all_to_all x1, blocking collectives, total_sum(): lax.all_to_all(spread, axes, 0, 0, axis_index_groups=groups)  9.89 us
    ppermute x5, starting transfers between devices, sum_over(): total = total + lax.ppermute(value, axis, pairs)  9.26 us
    pallas_call x1, Pallas kernels, body(): call(norm_kernel, [jax.ShapeDtypeStruct((y_local, width), F32), jax.Shape...  4.86 us
    ppermute x1, waiting for transfers between devices, total_sum(): other = lax.ppermute(mine.astype(BF16), 'row', swap)  3.86 us
    pallas_call x1, Pallas kernels, body(): call(finish_kernel, jax.ShapeDtypeStruct(slab_shape, BF16), 1 << 30, [plt...  2.97 us
    ppermute x5, waiting for transfers between devices, sum_over(): total = total + lax.ppermute(value, axis, pairs)  2.69 us
    pallas_call x1, Pallas kernels, body(): call(functools.partial(outer_kernel, mean_x, mean_y), jax.ShapeDtypeStruc...  2.3 us
  transfers between devices with their start and end apart: 6, of which 3 were waited for; matrix products, arithmetic and copies ran while one was open for 0% of the time, Pallas kernels for 3%

profile of v6, /device:TPU:0, one launch (start us, length us, event | category | flops | bytes accessed | tf_op | source)
XLA Modules:
  0.0 52.0 jit_solution(313146341432449628)
XLA Ops:
  0.0 0.0 copy-start
  0.0 4.9 %shard_map.82 = (f32[64,128]{1,0:T(8,128)}, bf16[16,6,64,128]{3,2,1,0:T(8,128)(2,1)}) custom-call(bf16[16,6,64,128]{3,2,1,0:T(8,128)(2,1)} %bitcast.7, f32[1,128]{1,0:T(1,128)} %bitcast.8, bf16[128,128]{1,0:T(8,128)(2,1)} %first_hbm.1), custom_call_target="tpu_custom_call" | custom-call | flops 1073741824 | bytes 4194304 | tf_op jit(solution)/shard_map/pallas_call | solution.py:255
  4.9 5.1 %collective-permute-start.3 = (f32[64,128]{1,0:T(8,128)}, f32[64,128]{1,0:T(8,128)S(1)}, u32[]{:S(2)}, u32[]{:S(2)}) collective-permute-start(f32[64,128]{1,0:T(8,128)} %get-tuple-element.18), channel_id=1, source_target_pairs={{0,24},{4,28},{8,0},{12,4},{16,8},{20,12},{24,16},{28,20},{1,25},{... | collective-permute-start | bytes 98312 | tf_op jit(solution)/shard_map/ppermute | solution.py:211
  10.0 0.0 collective-permute-start.2
  10.0 1.0 %collective-permute-start.1 = (f32[64,128]{1,0:T(8,128)}, f32[64,128]{1,0:T(8,128)S(1)}, u32[]{:S(2)}, u32[]{:S(2)}) collective-permute-start(f32[64,128]{1,0:T(8,128)} %get-tuple-element.18), channel_id=1, source_target_pairs={{0,8},{4,12},{8,16},{12,20},{16,24},{20,28},{24,0},{28,4},{1,9},{5... | collective-permute-start | bytes 98312 | tf_op jit(solution)/shard_map/ppermute | solution.py:211
  11.0 0.0 copy-done
  11.0 0.0 copy-start.3
  11.0 1.4 %copy-done.3 = bf16[16,6,64,128]{3,2,1,0:T(8,128)(2,1)S(1)} copy-done((bf16[16,6,64,128]{3,2,1,0:T(8,128)(2,1)S(1)}, bf16[16,6,64,128]{3,2,1,0:T(8,128)(2,1)}, u32[]{:S(2)}) %copy-start.3) | copy-done | bytes 1572888
  12.4 0.0 copy-start.4
  12.4 0.0 copy-start.5
  12.4 0.0 copy-start.6
  12.4 0.0 copy-start.1
  12.4 1.0 %shard_map.83 = f32[16,128]{1,0:T(8,128)S(1)} custom-call(bf16[16,6,64,128]{3,2,1,0:T(8,128)(2,1)S(1)} %copy-done.3, bf16[128,128]{1,0:T(8,128)(2,1)S(1)} %copy-done), custom_call_target="tpu_custom_call" | custom-call | flops 1073741824 | bytes 4194304 | tf_op jit(solution)/shard_map/pallas_call | solution.py:270
  13.4 1.6 %collective-permute-start = (f32[16,128]{1,0:T(8,128)S(1)}, f32[16,128]{1,0:T(8,128)S(1)}, u32[]{:S(2)}, u32[]{:S(2)}) collective-permute-start(f32[16,128]{1,0:T(8,128)S(1)} %shard_map.83), channel_id=1, source_target_pairs={{0,2},{2,0},{1,3},{3,1},{4,6},{6,4},{5,7},{7,5},{8,10},{10,8},{9,1... | collective-permute-start | bytes 24584 | tf_op jit(solution)/shard_map/ppermute | solution.py:211
  15.0 0.0 copy-done.4
  15.0 0.0 copy-done.5
  15.0 0.0 collective-permute-done.3
  15.1 0.0 collective-permute-done.2
  15.1 0.8 %collective-permute-done.1 = f32[64,128]{1,0:T(8,128)S(1)} collective-permute-done((f32[64,128]{1,0:T(8,128)}, f32[64,128]{1,0:T(8,128)S(1)}, u32[]{:S(2)}, u32[]{:S(2)}) %collective-permute-start.1) | collective-permute-done | bytes 32800 | tf_op jit(solution)/shard_map/ppermute | solution.py:211
  15.9 0.0 copy-done.6
  15.9 1.6 %collective-permute-start.4 = (f32[64,128]{1,0:T(8,128)S(1)}, f32[64,128]{1,0:T(8,128)S(1)}, u32[]{:S(2)}, u32[]{:S(2)}) collective-permute-start(f32[64,128]{1,0:T(8,128)S(1)} %add_add_fusion), channel_id=1, source_target_pairs={{0,4},{4,0},{8,12},{12,8},{16,20},{20,16},{24,28},{28,24},{1,5},{5... | collective-permute-start | bytes 98312 | tf_op jit(solution)/shard_map/ppermute | solution.py:211
  17.5 0.0 copy-done.1
  17.5 0.5 %shard_map.84.value_ref = bf16[16,64,768]{2,1,0:T(8,128)(2,1)S(1)} custom-call(bf16[16,6,64,128]{3,2,1,0:T(8,128)(2,1)S(1)} %copy-done.3, bf16[128,128]{1,0:T(8,128)(2,1)S(1)} %copy-done.1), custom_call_target="tpu_custom_call" | custom-call | flops 1073741824 | bytes 4194304 | tf_op jit(solution)/shard_map/pallas_call | solution.py:271
  18.0 0.0 collective-permute-done
  18.1 1.8 %collective-permute-done.4 = f32[64,128]{1,0:T(8,128)S(1)} collective-permute-done((f32[64,128]{1,0:T(8,128)S(1)}, f32[64,128]{1,0:T(8,128)S(1)}, u32[]{:S(2)}, u32[]{:S(2)}) %collective-permute-start.4) | collective-permute-done | bytes 32800 | tf_op jit(solution)/shard_map/ppermute | solution.py:211
  19.9 2.3 %shard_map.85 = bf16[256,768]{1,0:T(8,128)(2,1)S(1)} custom-call(f32[16,128]{1,0:T(8,128)S(1)} %add.18.sum_x_ref, f32[64,128]{1,0:T(8,128)S(1)} %add.22.sum_y_ref, bf16[128,128]{1,0:T(8,128)(2,1)S(1)} %get-tuple-element.33.key_x_ref, bf16[128,128]{1,0:T(8,128)(2,1)S(1)} %get-tuple-element.30.key_y_ref, bf16[16,64,768]{2,1,0:T(8,128)(2,1)S(1)} %shard_map.84.value_ref), custom_call_target="tpu_custom_call" | custom-call | flops 1073741824 | bytes 4194304 | tf_op jit(solution)/shard_map/pallas_call | solution.py:276
  22.2 11.2 %all_to_all.10 = bf16[8,32,768]{2,1,0:T(8,128)(2,1)S(1)} all-to-all(bf16[8,32,768]{2,1,0:T(8,128)(2,1)S(1)} %bitcast.5), channel_id=1, replica_groups={{0,2,4,6,8,10,12,14},{16,18,20,22,24,26,28,30},{1,3,5,7,9,11,13,15},{17..., dimensions={0} | all-to-all | bytes 786432 | tf_op jit(solution)/shard_map/all_to_all | solution.py:237
  33.4 0.1 convert_reduce_fusion
  33.4 0.0 copy-start.2
  33.5 1.5 %collective-permute-start.5 = (bf16[32,768]{1,0:T(8,128)(2,1)S(1)}, bf16[32,768]{1,0:T(8,128)(2,1)S(1)}, u32[]{:S(2)}, u32[]{:S(2)}) collective-permute-start(bf16[32,768]{1,0:T(8,128)(2,1)S(1)} %convert_element_type.13), channel_id=1, source_target_pairs={{0,16},{4,20},{8,24},{12,28},{16,0},{20,4},{24,8},{28,12},{1,17},{... | collective-permute-start | bytes 147464 | tf_op jit(solution)/shard_map/ppermute | solution.py:241
  34.9 0.3 shard_map.86
  35.2 3.9 %collective-permute-done.5 = bf16[32,768]{1,0:T(8,128)(2,1)S(1)} collective-permute-done((bf16[32,768]{1,0:T(8,128)(2,1)S(1)}, bf16[32,768]{1,0:T(8,128)(2,1)S(1)}, u32[]{:S(2)}, u32[]{:S(2)}) %collective-permute-start.5) | collective-permute-done | bytes 49184 | tf_op jit(solution)/shard_map/ppermute | solution.py:241
  39.1 9.9 %all_to_all.11 = bf16[8,32,768]{2,1,0:T(8,128)(2,1)S(1)} all-to-all(bf16[8,32,768]{2,1,0:T(8,128)(2,1)S(1)} %broadcast_in_dim.3), channel_id=1, replica_groups={{0,2,4,6,8,10,12,14},{16,18,20,22,24,26,28,30},{1,3,5,7,9,11,13,15},{17..., dimensions={0} | all-to-all | bytes 786432 | tf_op jit(solution)/shard_map/all_to_all | solution.py:245
  49.0 0.0 copy-done.2
  49.0 3.0 %shard_map.87 = bf16[16,6,64,128]{3,2,1,0:T(8,128)(2,1)} custom-call(bf16[128,256]{1,0:T(8,128)(2,1)S(1)} %get-tuple-element.26.left_ref, f32[16,2048]{1,0:T(8,128)S(1)} %get-tuple-element.27.rows_ref, bf16[256,768]{1,0:T(8,128)(2,1)S(1)} %bitcast.6, bf16[128,128]{1,0:T(8,128)(2,1)S(1)} %copy-done.2), custom_call_target="tpu_custom_call" | custom-call | flops 1073741824 | bytes 4194304 | tf_op jit(solution)/shard_map/pallas_call | solution.py:291
  (7 shorter events, 0.1 us)
Async XLA Ops:
  0.0 11.0 %copy-start = (bf16[128,128]{1,0:T(8,128)(2,1)S(1)}, bf16[128,128]{1,0:T(8,128)(2,1)}, u32[]{:S(2)}) copy-start(bf16[128,128]{1,0:T(8,128)(2,1)} %first_ref.1) | copy-start | bytes 98308
  4.9 10.2 %collective-permute-start.3 = (f32[64,128]{1,0:T(8,128)}, f32[64,128]{1,0:T(8,128)S(1)}, u32[]{:S(2)}, u32[]{:S(2)}) collective-permute-start(f32[64,128]{1,0:T(8,128)} %get-tuple-element.18), channel_id=1, source_target_pairs={{0,24},{4,28},{8,0},{12,4},{16,8},{20,12},{24,16},{28,20},{1,25},{... | collective-permute-start | bytes 98312 | tf_op jit(solution)/shard_map/ppermute | solution.py:211
  10.0 5.1 %collective-permute-start.2 = (f32[64,128]{1,0:T(8,128)}, f32[64,128]{1,0:T(8,128)S(1)}, u32[]{:S(2)}, u32[]{:S(2)}) collective-permute-start(f32[64,128]{1,0:T(8,128)} %get-tuple-element.18), channel_id=1, source_target_pairs={{0,16},{4,20},{8,24},{12,28},{16,0},{20,4},{24,8},{28,12},{1,17},{... | collective-permute-start | bytes 98312 | tf_op jit(solution)/shard_map/ppermute | solution.py:211
  10.0 5.9 %collective-permute-start.1 = (f32[64,128]{1,0:T(8,128)}, f32[64,128]{1,0:T(8,128)S(1)}, u32[]{:S(2)}, u32[]{:S(2)}) collective-permute-start(f32[64,128]{1,0:T(8,128)} %get-tuple-element.18), channel_id=1, source_target_pairs={{0,8},{4,12},{8,16},{12,20},{16,24},{20,28},{24,0},{28,4},{1,9},{5... | collective-permute-start | bytes 98312 | tf_op jit(solution)/shard_map/ppermute | solution.py:211
  11.0 1.4 %copy-start.3 = (bf16[16,6,64,128]{3,2,1,0:T(8,128)(2,1)S(1)}, bf16[16,6,64,128]{3,2,1,0:T(8,128)(2,1)}, u32[]{:S(2)}) copy-start(bf16[16,6,64,128]{3,2,1,0:T(8,128)(2,1)} %get-tuple-element.17.normed_ref) | copy-start | bytes 4718596
  12.4 2.6 %copy-start.4 = (bf16[128,256]{1,0:T(8,128)(2,1)S(1)}, bf16[128,256]{1,0:T(8,128)(2,1)}, u32[]{:S(2)}) copy-start(bf16[128,256]{1,0:T(8,128)(2,1)} %param.13) | copy-start | bytes 196612
  12.4 2.6 %copy-start.5 = (bf16[128,256]{1,0:T(8,128)(2,1)S(1)}, bf16[128,256]{1,0:T(8,128)(2,1)}, u32[]{:S(2)}) copy-start(bf16[128,256]{1,0:T(8,128)(2,1)} %param.11) | copy-start | bytes 196612
  12.4 3.5 %copy-start.6 = (f32[64,128]{1,0:T(8,128)S(1)}, f32[64,128]{1,0:T(8,128)}, u32[]{:S(2)}) copy-start(f32[64,128]{1,0:T(8,128)} %get-tuple-element.18) | copy-start | bytes 98308
  12.4 5.1 %copy-start.1 = (bf16[128,128]{1,0:T(8,128)(2,1)S(1)}, bf16[128,128]{1,0:T(8,128)(2,1)}, u32[]{:S(2)}) copy-start(bf16[128,128]{1,0:T(8,128)(2,1)} %weight_ref.2) | copy-start | bytes 98308
  13.4 4.6 %collective-permute-start = (f32[16,128]{1,0:T(8,128)S(1)}, f32[16,128]{1,0:T(8,128)S(1)}, u32[]{:S(2)}, u32[]{:S(2)}) collective-permute-start(f32[16,128]{1,0:T(8,128)S(1)} %shard_map.83), channel_id=1, source_target_pairs={{0,2},{2,0},{1,3},{3,1},{4,6},{6,4},{5,7},{7,5},{8,10},{10,8},{9,1... | collective-permute-start | bytes 24584 | tf_op jit(solution)/shard_map/ppermute | solution.py:211
  15.9 4.0 %collective-permute-start.4 = (f32[64,128]{1,0:T(8,128)S(1)}, f32[64,128]{1,0:T(8,128)S(1)}, u32[]{:S(2)}, u32[]{:S(2)}) collective-permute-start(f32[64,128]{1,0:T(8,128)S(1)} %add_add_fusion), channel_id=1, source_target_pairs={{0,4},{4,0},{8,12},{12,8},{16,20},{20,16},{24,28},{28,24},{1,5},{5... | collective-permute-start | bytes 98312 | tf_op jit(solution)/shard_map/ppermute | solution.py:211
  33.4 15.5 %copy-start.2 = (bf16[128,128]{1,0:T(8,128)(2,1)S(1)}, bf16[128,128]{1,0:T(8,128)(2,1)}, u32[]{:S(2)}) copy-start(bf16[128,128]{1,0:T(8,128)(2,1)} %weight_ref.3) | copy-start | bytes 98308
  33.5 5.6 %collective-permute-start.5 = (bf16[32,768]{1,0:T(8,128)(2,1)S(1)}, bf16[32,768]{1,0:T(8,128)(2,1)S(1)}, u32[]{:S(2)}, u32[]{:S(2)}) collective-permute-start(bf16[32,768]{1,0:T(8,128)(2,1)S(1)} %convert_element_type.13), channel_id=1, source_target_pairs={{0,16},{4,20},{8,24},{12,28},{16,0},{20,4},{24,8},{28,12},{1,17},{... | collective-permute-start | bytes 147464 | tf_op jit(solution)/shard_map/ppermute | solution.py:241

commit v7 on v6

--- a/solution.py
+++ b/solution.py
@@ -14,7 +14,7 @@
 GELU_A = 0.7978845608028654
 GELU_B = GELU_A * 0.044715
 VMEM_LIMIT = 48 * 1024 * 1024
-CHUNKS = 4
+CHUNKS = 2
 CUTS = (0, 2, 8, 14, 16)
 GROUP = 8
 WIDE_GROUP = 16

time: 52.2 us -> 52.2 us (level)
  transfers between devices with their start and end apart: 6 -> 6, of which waited for: 3 -> 3; matrix products, arithmetic and copies ran while one was open for 0% -> 0% of each run, Pallas kernels for 3% -> 4%
where the time goes in v7:
time: 52.2 us; the launch traced here: 52 us
  blocking collectives  21.1 us (40%)
  Pallas kernels  12 us (23%)
  starting transfers between devices  10.7 us (20%)
  waiting for transfers between devices  6.54 us (13%)
  local copies, waits for them, and re-layouts  1.48 us (3%)
    all_to_all x1, blocking collectives, total_sum(): lax.all_to_all(part.reshape(n, rows // n, lanes), axes, 0, 0, axis_index_...  11.2 us
    all_to_all x1, blocking collectives, total_sum(): lax.all_to_all(spread, axes, 0, 0, axis_index_groups=groups)  9.89 us
    ppermute x5, starting transfers between devices, sum_over(): total = total + lax.ppermute(value, axis, pairs)  9.27 us
    pallas_call x1, Pallas kernels, body(): call(norm_kernel, [jax.ShapeDtypeStruct((y_local, width), F32), jax.Shape...  4.86 us
    ppermute x1, waiting for transfers between devices, total_sum(): other = lax.ppermute(mine.astype(BF16), 'row', swap)  3.86 us
    pallas_call x1, Pallas kernels, body(): call(finish_kernel, jax.ShapeDtypeStruct(slab_shape, BF16), 1 << 30, [plt...  2.97 us
    ppermute x5, waiting for transfers between devices, sum_over(): total = total + lax.ppermute(value, axis, pairs)  2.68 us
    pallas_call x1, Pallas kernels, body(): call(functools.partial(outer_kernel, mean_x, mean_y), jax.ShapeDtypeStruc...  2.3 us
  transfers between devices with their start and end apart: 6, of which 3 were waited for; matrix products, arithmetic and copies ran while one was open for 0% of the time, Pallas kernels for 4%

profile of v7, /device:TPU:0, one launch (start us, length us, event | category | flops | bytes accessed | tf_op | source)
XLA Modules:
  0.0 52.0 jit_solution(13564528111338199757)
XLA Ops:
  0.0 0.0 copy-start
  0.0 4.9 %shard_map.82 = (f32[64,128]{1,0:T(8,128)}, bf16[16,6,64,128]{3,2,1,0:T(8,128)(2,1)}) custom-call(bf16[16,6,64,128]{3,2,1,0:T(8,128)(2,1)} %bitcast.7, f32[1,128]{1,0:T(1,128)} %bitcast.8, bf16[128,128]{1,0:T(8,128)(2,1)} %first_hbm.1), custom_call_target="tpu_custom_call" | custom-call | flops 1073741824 | bytes 4194304 | tf_op jit(solution)/shard_map/pallas_call | solution.py:255
  4.9 5.1 %collective-permute-start.3 = (f32[64,128]{1,0:T(8,128)}, f32[64,128]{1,0:T(8,128)S(1)}, u32[]{:S(2)}, u32[]{:S(2)}) collective-permute-start(f32[64,128]{1,0:T(8,128)} %get-tuple-element.18), channel_id=1, source_target_pairs={{0,24},{4,28},{8,0},{12,4},{16,8},{20,12},{24,16},{28,20},{1,25},{... | collective-permute-start | bytes 98312 | tf_op jit(solution)/shard_map/ppermute | solution.py:211
  10.0 0.0 collective-permute-start.2
  10.0 1.0 %collective-permute-start.1 = (f32[64,128]{1,0:T(8,128)}, f32[64,128]{1,0:T(8,128)S(1)}, u32[]{:S(2)}, u32[]{:S(2)}) collective-permute-start(f32[64,128]{1,0:T(8,128)} %get-tuple-element.18), channel_id=1, source_target_pairs={{0,8},{4,12},{8,16},{12,20},{16,24},{20,28},{24,0},{28,4},{1,9},{5... | collective-permute-start | bytes 98312 | tf_op jit(solution)/shard_map/ppermute | solution.py:211
  11.0 0.0 copy-done
  11.0 0.0 copy-start.3
  11.0 1.4 %copy-done.3 = bf16[16,6,64,128]{3,2,1,0:T(8,128)(2,1)S(1)} copy-done((bf16[16,6,64,128]{3,2,1,0:T(8,128)(2,1)S(1)}, bf16[16,6,64,128]{3,2,1,0:T(8,128)(2,1)}, u32[]{:S(2)}) %copy-start.3) | copy-done | bytes 1572888
  12.4 0.0 copy-start.4
  12.4 0.0 copy-start.5
  12.4 0.0 copy-start.6
  12.4 0.0 copy-start.1
  12.4 1.0 %shard_map.83 = f32[16,128]{1,0:T(8,128)S(1)} custom-call(bf16[16,6,64,128]{3,2,1,0:T(8,128)(2,1)S(1)} %copy-done.3, bf16[128,128]{1,0:T(8,128)(2,1)S(1)} %copy-done), custom_call_target="tpu_custom_call" | custom-call | flops 1073741824 | bytes 4194304 | tf_op jit(solution)/shard_map/pallas_call | solution.py:270
  13.4 1.6 %collective-permute-start = (f32[16,128]{1,0:T(8,128)S(1)}, f32[16,128]{1,0:T(8,128)S(1)}, u32[]{:S(2)}, u32[]{:S(2)}) collective-permute-start(f32[16,128]{1,0:T(8,128)S(1)} %shard_map.83), channel_id=1, source_target_pairs={{0,2},{2,0},{1,3},{3,1},{4,6},{6,4},{5,7},{7,5},{8,10},{10,8},{9,1... | collective-permute-start | bytes 24584 | tf_op jit(solution)/shard_map/ppermute | solution.py:211
  15.0 0.0 copy-done.4
  15.0 0.0 copy-done.5
  15.0 0.0 collective-permute-done.3
  15.1 0.0 collective-permute-done.2
  15.1 0.8 %collective-permute-done.1 = f32[64,128]{1,0:T(8,128)S(1)} collective-permute-done((f32[64,128]{1,0:T(8,128)}, f32[64,128]{1,0:T(8,128)S(1)}, u32[]{:S(2)}, u32[]{:S(2)}) %collective-permute-start.1) | collective-permute-done | bytes 32800 | tf_op jit(solution)/shard_map/ppermute | solution.py:211
  15.9 0.0 copy-done.6
  15.9 1.6 %collective-permute-start.4 = (f32[64,128]{1,0:T(8,128)S(1)}, f32[64,128]{1,0:T(8,128)S(1)}, u32[]{:S(2)}, u32[]{:S(2)}) collective-permute-start(f32[64,128]{1,0:T(8,128)S(1)} %add_add_fusion), channel_id=1, source_target_pairs={{0,4},{4,0},{8,12},{12,8},{16,20},{20,16},{24,28},{28,24},{1,5},{5... | collective-permute-start | bytes 98312 | tf_op jit(solution)/shard_map/ppermute | solution.py:211
  17.5 0.0 copy-done.1
  17.5 0.6 %shard_map.84.value_ref = bf16[16,64,768]{2,1,0:T(8,128)(2,1)S(1)} custom-call(bf16[16,6,64,128]{3,2,1,0:T(8,128)(2,1)S(1)} %copy-done.3, bf16[128,128]{1,0:T(8,128)(2,1)S(1)} %copy-done.1), custom_call_target="tpu_custom_call" | custom-call | flops 1073741824 | bytes 4194304 | tf_op jit(solution)/shard_map/pallas_call | solution.py:271
  18.0 0.0 collective-permute-done
  18.1 1.8 %collective-permute-done.4 = f32[64,128]{1,0:T(8,128)S(1)} collective-permute-done((f32[64,128]{1,0:T(8,128)S(1)}, f32[64,128]{1,0:T(8,128)S(1)}, u32[]{:S(2)}, u32[]{:S(2)}) %collective-permute-start.4) | collective-permute-done | bytes 32800 | tf_op jit(solution)/shard_map/ppermute | solution.py:211
  19.9 2.3 %shard_map.85 = bf16[256,768]{1,0:T(8,128)(2,1)S(1)} custom-call(f32[16,128]{1,0:T(8,128)S(1)} %add.18.sum_x_ref, f32[64,128]{1,0:T(8,128)S(1)} %add.22.sum_y_ref, bf16[128,128]{1,0:T(8,128)(2,1)S(1)} %get-tuple-element.33.key_x_ref, bf16[128,128]{1,0:T(8,128)(2,1)S(1)} %get-tuple-element.30.key_y_ref, bf16[16,64,768]{2,1,0:T(8,128)(2,1)S(1)} %shard_map.84.value_ref), custom_call_target="tpu_custom_call" | custom-call | flops 1073741824 | bytes 4194304 | tf_op jit(solution)/shard_map/pallas_call | solution.py:276
  22.2 11.2 %all_to_all.10 = bf16[8,32,768]{2,1,0:T(8,128)(2,1)S(1)} all-to-all(bf16[8,32,768]{2,1,0:T(8,128)(2,1)S(1)} %bitcast.5), channel_id=1, replica_groups={{0,2,4,6,8,10,12,14},{16,18,20,22,24,26,28,30},{1,3,5,7,9,11,13,15},{17..., dimensions={0} | all-to-all | bytes 786432 | tf_op jit(solution)/shard_map/all_to_all | solution.py:237
  33.4 0.1 convert_reduce_fusion
  33.4 0.0 copy-start.2
  33.5 1.5 %collective-permute-start.5 = (bf16[32,768]{1,0:T(8,128)(2,1)S(1)}, bf16[32,768]{1,0:T(8,128)(2,1)S(1)}, u32[]{:S(2)}, u32[]{:S(2)}) collective-permute-start(bf16[32,768]{1,0:T(8,128)(2,1)S(1)} %convert_element_type.13), channel_id=1, source_target_pairs={{0,16},{4,20},{8,24},{12,28},{16,0},{20,4},{24,8},{28,12},{1,17},{... | collective-permute-start | bytes 147464 | tf_op jit(solution)/shard_map/ppermute | solution.py:241
  34.9 0.3 shard_map.86
  35.2 3.9 %collective-permute-done.5 = bf16[32,768]{1,0:T(8,128)(2,1)S(1)} collective-permute-done((bf16[32,768]{1,0:T(8,128)(2,1)S(1)}, bf16[32,768]{1,0:T(8,128)(2,1)S(1)}, u32[]{:S(2)}, u32[]{:S(2)}) %collective-permute-start.5) | collective-permute-done | bytes 49184 | tf_op jit(solution)/shard_map/ppermute | solution.py:241
  39.1 9.9 %all_to_all.11 = bf16[8,32,768]{2,1,0:T(8,128)(2,1)S(1)} all-to-all(bf16[8,32,768]{2,1,0:T(8,128)(2,1)S(1)} %broadcast_in_dim.3), channel_id=1, replica_groups={{0,2,4,6,8,10,12,14},{16,18,20,22,24,26,28,30},{1,3,5,7,9,11,13,15},{17..., dimensions={0} | all-to-all | bytes 786432 | tf_op jit(solution)/shard_map/all_to_all | solution.py:245
  49.0 0.0 copy-done.2
  49.0 3.0 %shard_map.87 = bf16[16,6,64,128]{3,2,1,0:T(8,128)(2,1)} custom-call(bf16[128,256]{1,0:T(8,128)(2,1)S(1)} %get-tuple-element.26.left_ref, f32[16,2048]{1,0:T(8,128)S(1)} %get-tuple-element.27.rows_ref, bf16[256,768]{1,0:T(8,128)(2,1)S(1)} %bitcast.6, bf16[128,128]{1,0:T(8,128)(2,1)S(1)} %copy-done.2), custom_call_target="tpu_custom_call" | custom-call | flops 1073741824 | bytes 4194304 | tf_op jit(solution)/shard_map/pallas_call | solution.py:291
  (7 shorter events, 0.1 us)
Async XLA Ops:
  0.0 11.0 %copy-start = (bf16[128,128]{1,0:T(8,128)(2,1)S(1)}, bf16[128,128]{1,0:T(8,128)(2,1)}, u32[]{:S(2)}) copy-start(bf16[128,128]{1,0:T(8,128)(2,1)} %first_ref.1) | copy-start | bytes 98308
  4.9 10.2 %collective-permute-start.3 = (f32[64,128]{1,0:T(8,128)}, f32[64,128]{1,0:T(8,128)S(1)}, u32[]{:S(2)}, u32[]{:S(2)}) collective-permute-start(f32[64,128]{1,0:T(8,128)} %get-tuple-element.18), channel_id=1, source_target_pairs={{0,24},{4,28},{8,0},{12,4},{16,8},{20,12},{24,16},{28,20},{1,25},{... | collective-permute-start | bytes 98312 | tf_op jit(solution)/shard_map/ppermute | solution.py:211
  10.0 5.1 %collective-permute-start.2 = (f32[64,128]{1,0:T(8,128)}, f32[64,128]{1,0:T(8,128)S(1)}, u32[]{:S(2)}, u32[]{:S(2)}) collective-permute-start(f32[64,128]{1,0:T(8,128)} %get-tuple-element.18), channel_id=1, source_target_pairs={{0,16},{4,20},{8,24},{12,28},{16,0},{20,4},{24,8},{28,12},{1,17},{... | collective-permute-start | bytes 98312 | tf_op jit(solution)/shard_map/ppermute | solution.py:211
  10.0 5.9 %collective-permute-start.1 = (f32[64,128]{1,0:T(8,128)}, f32[64,128]{1,0:T(8,128)S(1)}, u32[]{:S(2)}, u32[]{:S(2)}) collective-permute-start(f32[64,128]{1,0:T(8,128)} %get-tuple-element.18), channel_id=1, source_target_pairs={{0,8},{4,12},{8,16},{12,20},{16,24},{20,28},{24,0},{28,4},{1,9},{5... | collective-permute-start | bytes 98312 | tf_op jit(solution)/shard_map/ppermute | solution.py:211
  11.0 1.4 %copy-start.3 = (bf16[16,6,64,128]{3,2,1,0:T(8,128)(2,1)S(1)}, bf16[16,6,64,128]{3,2,1,0:T(8,128)(2,1)}, u32[]{:S(2)}) copy-start(bf16[16,6,64,128]{3,2,1,0:T(8,128)(2,1)} %get-tuple-element.17.normed_ref) | copy-start | bytes 4718596
  12.4 2.6 %copy-start.4 = (bf16[128,256]{1,0:T(8,128)(2,1)S(1)}, bf16[128,256]{1,0:T(8,128)(2,1)}, u32[]{:S(2)}) copy-start(bf16[128,256]{1,0:T(8,128)(2,1)} %param.13) | copy-start | bytes 196612
  12.4 2.6 %copy-start.5 = (bf16[128,256]{1,0:T(8,128)(2,1)S(1)}, bf16[128,256]{1,0:T(8,128)(2,1)}, u32[]{:S(2)}) copy-start(bf16[128,256]{1,0:T(8,128)(2,1)} %param.11) | copy-start | bytes 196612
  12.4 3.5 %copy-start.6 = (f32[64,128]{1,0:T(8,128)S(1)}, f32[64,128]{1,0:T(8,128)}, u32[]{:S(2)}) copy-start(f32[64,128]{1,0:T(8,128)} %get-tuple-element.18) | copy-start | bytes 98308
  12.4 5.1 %copy-start.1 = (bf16[128,128]{1,0:T(8,128)(2,1)S(1)}, bf16[128,128]{1,0:T(8,128)(2,1)}, u32[]{:S(2)}) copy-start(bf16[128,128]{1,0:T(8,128)(2,1)} %weight_ref.2) | copy-start | bytes 98308
  13.4 4.6 %collective-permute-start = (f32[16,128]{1,0:T(8,128)S(1)}, f32[16,128]{1,0:T(8,128)S(1)}, u32[]{:S(2)}, u32[]{:S(2)}) collective-permute-start(f32[16,128]{1,0:T(8,128)S(1)} %shard_map.83), channel_id=1, source_target_pairs={{0,2},{2,0},{1,3},{3,1},{4,6},{6,4},{5,7},{7,5},{8,10},{10,8},{9,1... | collective-permute-start | bytes 24584 | tf_op jit(solution)/shard_map/ppermute | solution.py:211
  15.9 4.0 %collective-permute-start.4 = (f32[64,128]{1,0:T(8,128)S(1)}, f32[64,128]{1,0:T(8,128)S(1)}, u32[]{:S(2)}, u32[]{:S(2)}) collective-permute-start(f32[64,128]{1,0:T(8,128)S(1)} %add_add_fusion), channel_id=1, source_target_pairs={{0,4},{4,0},{8,12},{12,8},{16,20},{20,16},{24,28},{28,24},{1,5},{5... | collective-permute-start | bytes 98312 | tf_op jit(solution)/shard_map/ppermute | solution.py:211
  33.4 15.5 %copy-start.2 = (bf16[128,128]{1,0:T(8,128)(2,1)S(1)}, bf16[128,128]{1,0:T(8,128)(2,1)}, u32[]{:S(2)}) copy-start(bf16[128,128]{1,0:T(8,128)(2,1)} %weight_ref.3) | copy-start | bytes 98308
  33.5 5.6 %collective-permute-start.5 = (bf16[32,768]{1,0:T(8,128)(2,1)S(1)}, bf16[32,768]{1,0:T(8,128)(2,1)S(1)}, u32[]{:S(2)}, u32[]{:S(2)}) collective-permute-start(bf16[32,768]{1,0:T(8,128)(2,1)S(1)} %convert_element_type.13), channel_id=1, source_target_pairs={{0,16},{4,20},{8,24},{12,28},{16,0},{20,4},{24,8},{28,12},{1,17},{... | collective-permute-start | bytes 147464 | tf_op jit(solution)/shard_map/ppermute | solution.py:241
